TPU v7x, 512 devices: a whole 4x8x8 slice. The times are simulated.
512 devices in a mesh: src: 32 (over z_lo, x, core), tgt: 16 (over z_hi, y).
Axes of the slice: x: 4, y: 8, z: 8 (z_hi: 2, z_lo: 4; z = z_hi * 4 + z_lo), core: 2. Of those that a mesh axis runs over, the one named last changes fastest.
Arguments:
- src_embed: bfloat16 [8192, 1024], P('src', 'tgt'), as said below
- tgt_embed: bfloat16 [4096, 1024], P('tgt', 'src')
- src_near: int32 [8192, 16], P('src'), may hold values from 0 to 4095
- tgt_near: int32 [4096, 16], P('tgt'), may hold values from 0 to 8191
Outputs:
- margin: bfloat16 [8192, 4096], P('src', 'tgt')
- src_average: float32 [8192], P('src')
- tgt_average: float32 [4096], P('tgt')
Inputs may be any that keep to these rules, and one draw needn't show every extreme that they name: `src_embed`: every embedding is a sentence-specific multiple of one direction shared by both languages plus independent variation of comparable size, so that all cosines of the draw are positive.
All inputs are finite; a program needn't handle non-finite values.
Results may differ from a plain program's by a relative error of at most 0.001.
Values may be sent and summed in bfloat16 or wider, within the bound.
No kernel may reach another device: no remote copies, remote signals or barrier semaphores. Data moves between devices by JAX's collectives and lax.ppermute only.
A program may use at most 64 MiB of HBM per device.

v0:
```python
import jax
import jax.numpy as jnp
from jax import lax
from jax.sharding import PartitionSpec as P

EPSILON = 1e-06


def square_sums(values):
    wide = values.astype(jnp.float32)
    return jnp.sum(wide * wide, axis=1)


def local(src_embed, tgt_embed, src_near, tgt_near):
    src_index = lax.axis_index("src")
    tgt_index = lax.axis_index("tgt")
    source_rows = lax.all_gather(src_embed, "tgt", axis=1, tiled=True)
    src_count = source_rows.shape[0]
    tgt_count = tgt_embed.shape[0]
    near_count = src_near.shape[1]
    src_norm = jnp.sqrt(square_sums(source_rows) + EPSILON)
    contract = (((1,), (1,)), ((), ()))
    target_rows = lax.all_gather(tgt_embed, "src", axis=1, tiled=True)
    products = lax.dot_general(
        source_rows, target_rows, contract, preferred_element_type=jnp.float32
    )
    tgt_squares = square_sums(target_rows)
    tgt_norm = jnp.sqrt(tgt_squares + EPSILON)
    cosine_tile = products / (src_norm[:, None] * tgt_norm[None, :])
    local_targets = src_near - tgt_index * tgt_count
    local_sources = tgt_near - src_index * src_count
    target_iota = lax.broadcasted_iota(jnp.int32, (1, tgt_count), 1)
    source_iota = lax.broadcasted_iota(jnp.int32, (src_count, 1), 0)

    def add_neighbour(step, sums):
        row_sum, column_sum = sums
        wanted_target = lax.dynamic_slice_in_dim(local_targets, step, 1, 1)
        row_hits = wanted_target == target_iota
        row_sum = row_sum + jnp.sum(jnp.where(row_hits, cosine_tile, 0.0), axis=1)
        wanted_source = lax.dynamic_slice_in_dim(local_sources, step, 1, 1)
        column_hits = source_iota == wanted_source.reshape(1, tgt_count)
        column_sum = column_sum + jnp.sum(jnp.where(column_hits, cosine_tile, 0.0), axis=0)
        return (row_sum, column_sum)

    start_sums = (jnp.zeros((src_count,), jnp.float32), jnp.zeros((tgt_count,), jnp.float32))
    row_partial, column_partial = lax.fori_loop(0, near_count, add_neighbour, start_sums)
    src_average = lax.psum(row_partial, "tgt") / near_count
    tgt_average = lax.psum(column_partial, "src") / near_count
    margin = (cosine_tile / ((src_average[:, None] + tgt_average[None, :]) / 2.0)).astype(
        jnp.bfloat16
    )
    return (margin, src_average, tgt_average)


def solution(mesh):
    placed = (P("src", "tgt"), P("tgt", "src"), P("src", None), P("tgt", None))
    return jax.shard_map(
        local,
        mesh=mesh,
        in_specs=placed,
        out_specs=(P("src", "tgt"), P("src"), P("tgt")),
        check_vma=False,
    )
```

profile of v0, /device:TPU:8, one launch (start us, length us, event | category | flops | bytes accessed | tf_op | source)
XLA Modules:
  0.0 227.9 jit_solution(2381617098433261783)
XLA Ops:
  0.6 47.4 %all_gather.7 = bf16[256,1024]{0,1:T(8,128)(2,1)S(1)} all-gather(bf16[256,32]{0,1:T(8,128)(2,1)} %param.7), channel_id=1, replica_groups=mesh['src'=32,'tgt'=16] {'src'}, dimensions={1}, use_global_device_ids=true | all-gather | bytes 540672 | tf_op jit(solution)/shard_map/all_gather | solution.py:23
  48.0 0.0 copy-start
  48.0 0.2 multiply_reduce_fusion
  48.2 0.6 copy-done
  48.8 51.3 %all_gather.6 = bf16[256,1024]{0,1:T(8,128)(2,1)S(1)} all-gather(bf16[256,64]{0,1:T(8,128)(2,1)S(1)} %copy-done), channel_id=1, replica_groups=mesh['src'=32,'tgt'=16] {'tgt'}, dimensions={1}, use_global_device_ids=true | all-gather | bytes 557056 | tf_op jit(solution)/shard_map/all_gather | solution.py:17
  100.1 0.2 multiply_reduce_fusion.1
  100.2 0.0 copy-start.2
  100.2 0.3 multiply_divide_fusion
  100.6 0.0 copy-start.1
  100.6 0.4 copy-done.2
  101.0 0.3 copy-done.1
  101.3 4.0 %while.16 = (s32[]{:T(128)}, f32[256]{0:T(256)S(1)}, f32[256]{0:T(256)S(1)}, s32[256,16]{0,1:T(8,128)S(1)}, f32[256,256]{1,0:T(8,128)S(1)}, /*index=5*/s32[256,16]{0,1:T(8,128)S(1)}, s32[]{:T(128)}, s32[]{:T(128)}) while((s32[]{:T(128)}, f32[256]{0:T(256)S(1)}, f32[256]{0:T(256)S(1)}, s32[256,16]{0,1:T(8,128)S(1)}, ...), condition=%wide.region_5.6_spmd.clone, body=%wide.region_2.5_spmd.clone.sunk | while | flops 393731 | bytes 276583 | solution.py:46
  101.3 0.2 select_reduce_fusion.3
  101.6 0.2 select_reduce_fusion.3
  101.8 0.2 select_reduce_fusion.3
  102.1 0.2 select_reduce_fusion.3
  102.4 0.2 select_reduce_fusion.3
  102.6 0.2 select_reduce_fusion.3
  102.9 0.2 select_reduce_fusion.3
  103.1 0.2 select_reduce_fusion.3
  103.4 0.2 select_reduce_fusion.3
  103.6 0.2 select_reduce_fusion.3
  103.9 0.2 select_reduce_fusion.3
  104.1 0.2 select_reduce_fusion.3
  104.4 0.2 select_reduce_fusion.3
  104.6 0.2 select_reduce_fusion.3
  104.9 0.2 select_reduce_fusion.3
  105.1 0.2 select_reduce_fusion.3
  105.3 67.4 %psum.15 = f32[256]{0:T(256)S(1)} all-reduce(f32[256]{0:T(256)S(1)} %get-tuple-element.144), channel_id=1, replica_groups=mesh['src'=32,'tgt'=16] {'src'}, use_global_device_ids=true, to_apply=%region_7.8 | all-reduce | flops 256 | bytes 2048 | tf_op jit(solution)/shard_map/psum | solution.py:48
  172.7 0.0 copy-start.3
  172.7 54.4 %psum.14 = f32[256]{0:T(256)S(1)} all-reduce(f32[256]{0:T(256)S(1)} %get-tuple-element.143), channel_id=1, replica_groups=mesh['src'=32,'tgt'=16] {'tgt'}, use_global_device_ids=true, to_apply=%region_6.7 | all-reduce | flops 256 | bytes 2048 | tf_op jit(solution)/shard_map/psum | solution.py:47
  227.1 0.0 copy-start.4
  227.1 0.0 copy-done.3
  227.1 0.8 fusion.5
  227.9 0.0 copy-done.4
  (55 shorter events, 0.6 us)
Async XLA Ops:
  48.0 0.8 copy-start
  100.2 0.7 copy-start.2
  100.6 0.7 copy-start.1
  172.7 54.4 %copy-start.3 = (f32[256]{0:T(256)}, f32[256]{0:T(256)S(1)}, u32[]{:S(2)}) copy-start(f32[256]{0:T(256)S(1)} %broadcast_multiply_fusion) | copy-start | bytes 3076
  227.1 0.8 copy-start.4
where the time goes:
time: 228 us
  blocking collectives  220 us (96%)
  other arithmetic  4.33 us (2%)
    psum x1, blocking collectives, local(): tgt_average = lax.psum(column_partial, 'src') / near_count  67.4 us
    psum x1, blocking collectives, local(): src_average = lax.psum(row_partial, 'tgt') / near_count  54.4 us
    all_gather x1, blocking collectives, local(): source_rows = lax.all_gather(src_embed, 'tgt', axis=1, tiled=True)  51.3 us
    all_gather x1, blocking collectives, local(): target_rows = lax.all_gather(tgt_embed, 'src', axis=1, tiled=True)  47.4 us

commit v1 on v0

v1 whole, which is shorter than its diff:
```python
import jax
import jax.numpy as jnp
from jax import lax
from jax.experimental import pallas as pl
from jax.experimental.pallas import tpu as pltpu
from jax.sharding import PartitionSpec as P

EPSILON = 1e-06
LANES = 128
CORES = 2
MAJOR = (((0,), (0,)), ((), ()))


def spread(values, count):
    return jnp.broadcast_to(values[None], (count,) + values.shape)


def inverse_norms(values):
    wide = values.astype(jnp.float32)
    return lax.rsqrt(jnp.sum(wide * wide, axis=0, keepdims=True) + EPSILON)


def picked(cosines, index):
    total = jnp.zeros(index.shape, jnp.float32)
    for half in range(cosines.shape[1] // LANES):
        block = cosines[:, half * LANES : (half + 1) * LANES]
        found = jnp.take_along_axis(block, index & (LANES - 1), axis=1)
        total = total + jnp.where(index >> 7 == half, found, 0.0)
    return jnp.sum(total.T, axis=0, keepdims=True)


def tile_kernel(core_ref, s_ref, own_ref, other_ref, near_t_ref, near_s_ref, cos_ref, row_ref, col_ref):
    core = core_ref[0]
    parts, _, width, rows = s_ref.shape
    flat = (parts * width, rows)
    s_own = s_ref[:, pl.ds(core, 1)].reshape(flat)
    s_other = s_ref[:, pl.ds(1 - core, 1)].reshape(flat)
    t_own = own_ref[...].reshape(flat)
    t_other = other_ref[...].reshape(flat)
    s_scale = inverse_norms(jnp.concatenate([s_own, s_other], axis=0))
    t_scale = inverse_norms(jnp.concatenate([t_own, t_other], axis=0))

    def product(a, b):
        return lax.dot_general(a, b, MAJOR, preferred_element_type=jnp.float32)

    def column(scale):
        return jnp.broadcast_to(scale, (8, rows)).T[:, :1]

    cosines = product(s_own, t_own) + product(s_other, t_other)
    cosines = cosines * column(s_scale) * t_scale
    cos_ref[...] = cosines
    row_ref[...] = picked(cosines, near_t_ref[...])
    flipped = product(t_own, s_own) + product(t_other, s_other)
    flipped = flipped * column(t_scale) * s_scale
    col_ref[...] = picked(flipped, near_s_ref[...])


def local(src_embed, tgt_embed, src_near, tgt_near):
    src_index = lax.axis_index("src")
    tgt_index = lax.axis_index("tgt")
    core = src_index % CORES
    src_size = lax.axis_size("src")
    tgt_size = lax.axis_size("tgt")
    chips = src_size // CORES
    src_count, near_count = src_near.shape
    tgt_count = tgt_near.shape[0]
    pair = [(i, i ^ 1) for i in range(src_size)]
    same_core = [[q * CORES + c for q in range(chips)] for c in range(CORES)]

    def index_of(s, t):
        return s * tgt_size + t

    lines = [[index_of(q * CORES, t) for t in range(tgt_size)] for q in range(chips)]
    lines += [[index_of(q * CORES + 1, t) for q in range(chips)] for t in range(tgt_size)]

    def padded(near, start):
        return jnp.pad(near - start, ((0, 0), (0, LANES - near_count)), constant_values=-1)

    near_t = padded(src_near, tgt_index * tgt_count)
    near_s = padded(tgt_near, src_index * src_count)
    own = lax.all_to_all(
        spread(tgt_embed.T, chips), "src", 0, 0, axis_index_groups=same_core
    )
    own, src_part = lax.optimization_barrier((own, src_embed))
    other = lax.ppermute(own, "src", pair)
    source = lax.all_to_all(spread(src_part.T, tgt_size), "tgt", 0, 0)
    source = source.reshape(tgt_size, CORES, -1, src_count)
    vmem = pl.BlockSpec(memory_space=pltpu.VMEM)
    smem = pl.BlockSpec(memory_space=pltpu.SMEM)
    cosines, row, col = pl.pallas_call(
        tile_kernel,
        in_specs=[smem] + [vmem] * 5,
        out_specs=[vmem] * 3,
        out_shape=[
            jax.ShapeDtypeStruct((src_count, tgt_count), jnp.float32),
            jax.ShapeDtypeStruct((1, src_count), jnp.float32),
            jax.ShapeDtypeStruct((1, tgt_count), jnp.float32),
        ],
        compiler_params=pltpu.CompilerParams(vmem_limit_bytes=32 * 1024 * 1024),
        cost_estimate=pl.CostEstimate(flops=300_000_000, bytes_accessed=2**21, transcendentals=512),
    )(core.astype(jnp.int32).reshape(1), source, own, other, near_t, near_s)

    first = core == 0
    crossed = lax.ppermute(jnp.where(first, col, row), "src", pair)
    sums = jnp.where(
        first,
        jnp.concatenate([row, crossed], axis=0),
        jnp.broadcast_to(col + crossed, (2, tgt_count)),
    )
    parts = lax.all_to_all(spread(sums, chips), ("src", "tgt"), 0, 0, axis_index_groups=lines)
    averages = jnp.sum(parts, axis=0) / near_count
    kept = averages[0]
    crossed = lax.ppermute(averages[1], "src", pair)
    src_average = jnp.where(first, kept, crossed)
    tgt_average = jnp.where(first, crossed, kept)
    margin = (cosines / ((src_average[:, None] + tgt_average[None, :]) / 2.0)).astype(
        jnp.bfloat16
    )
    return (margin, src_average, tgt_average)


def solution(mesh):
    placed = (P("src", "tgt"), P("tgt", "src"), P("src", None), P("tgt", None))
    return jax.shard_map(
        local,
        mesh=mesh,
        in_specs=placed,
        out_specs=(P("src", "tgt"), P("src"), P("tgt")),
        check_vma=False,
    )
```

time: 228 us -> 81 us (0.36)
  the two profiles are of different devices: /device:TPU:8 before, /device:TPU:1 now
where the time goes in v1:
time: 81 us; the launch traced here: 80.4 us
  starting transfers between devices  31.5 us (39%)
  blocking collectives  30.4 us (38%)
  waiting for transfers between devices  12.6 us (16%)
  local copies, waits for them, and re-layouts  3.1 us (4%)
  Pallas kernels  1.18 us (1%)
  other arithmetic  0.85 us (1%)
    all_to_all x1, blocking collectives, local(): lax.all_to_all(spread(tgt_embed.T, chips), 'src', 0, 0, axis_index_groups...  19.7 us
    all_to_all x1, starting transfers between devices, local(): source = lax.all_to_all(spread(src_part.T, tgt_size), 'tgt', 0, 0)  12.8 us
    all_to_all x1, waiting for transfers between devices, local(): source = lax.all_to_all(spread(src_part.T, tgt_size), 'tgt', 0, 0)  10.8 us
    all_to_all x1, blocking collectives, local(): lax.all_to_all(spread(sums, chips), ('src', 'tgt'), 0, 0, axis_index_grou...  10.7 us
    ppermute x1, starting transfers between devices, local(): crossed = lax.ppermute(averages[1], 'src', pair)  8.6 us
    ppermute x1, starting transfers between devices, local(): crossed = lax.ppermute(jnp.where(first, col, row), 'src', pair)  5.75 us
    ppermute x1, starting transfers between devices, local(): other = lax.ppermute(own, 'src', pair)  4.32 us
  transfers between devices with their start and end apart: 4, of which 4 were waited for; matrix products, arithmetic and copies ran while one was open for 0% of the time, Pallas kernels for 0%

profile of v1, /device:TPU:1, one launch (start us, length us, event | category | flops | bytes accessed | tf_op | source)
XLA Modules:
  0.0 80.4 jit_solution(4878671604929088652)
XLA Ops:
  0.6 0.7 broadcast_in_dim.8
  1.4 0.0 copy-start
  1.4 19.7 %all_to_all.15.own_ref = bf16[16,32,256]{2,1,0:T(8,128)(2,1)S(1)} all-to-all(bf16[16,32,256]{2,1,0:T(8,128)(2,1)S(1)} %broadcast_in_dim.8), channel_id=1, replica_groups={{0,32,64,96,128,160,192,224,256,288,320,352,384,416,448,480},{16,48,80,..., dimensions={0} | all-to-all | bytes 524288 | tf_op jit(solution)/shard_map/all_to_all | solution.py:81
  21.1 0.0 copy-done
  21.1 0.8 %broadcast_in_dim.9 = bf16[16,64,256]{2,1,0:T(8,128)(2,1)} broadcast(bf16[64,256]{1,0:T(8,128)(2,1)S(1)} %bitcast.8), dimensions={1,2} | broadcast | bytes 557056 | tf_op jit(solution)/shard_map/broadcast_in_dim | solution.py:15
  21.9 0.0 copy-start.1
  21.9 12.8 %all-to-all-start.1 = ((bf16[16,64,256]{2,1,0:T(8,128)(2,1)}), bf16[16,64,256]{2,1,0:T(8,128)(2,1)S(1)}, u32[]{:S(2)}, u32[]{:S(2)}) async-start(bf16[16,64,256]{2,1,0:T(8,128)(2,1)} %broadcast_in_dim.9), calls=%async_computation.1 | async-start | bytes 1048576 | tf_op jit(solution)/shard_map/all_to_all | solution.py:86
  34.7 0.0 copy-done.1
  34.7 0.1 copy.14
  34.8 4.3 %collective-permute-start = (bf16[16,32,256]{2,1,0:T(8,128)(2,1)S(1)}, bf16[16,32,256]{2,1,0:T(8,128)(2,1)S(1)}, u32[]{:S(2)}, u32[]{:S(2)}) collective-permute-start(bf16[16,32,256]{2,1,0:T(8,128)(2,1)S(1)} %all_to_all.15.own_ref), channel_id=1, source_target_pairs={{0,16},{16,0},{32,48},{48,32},{64,80},{80,64},{96,112},{112,96},{1... | collective-permute-start | bytes 786440 | tf_op jit(solution)/shard_map/ppermute | solution.py:85
  39.2 0.0 copy-start.2
  39.2 0.7 copy-done.2
  39.9 0.1 copy.16
  40.1 0.2 collective-permute-done.other_ref
  40.3 10.8 %all-to-all-done.1 = bf16[16,64,256]{2,1,0:T(8,128)(2,1)S(1)} async-done(((bf16[16,64,256]{2,1,0:T(8,128)(2,1)}), bf16[16,64,256]{2,1,0:T(8,128)(2,1)S(1)}, u32[]{:S(2)}, u32[]{:S(2)}) %all-to-all-start.1) | async-done | bytes 524320 | tf_op jit(solution)/shard_map/all_to_all | solution.py:86
  51.1 1.2 %shard_map.67 = (f32[256,256]{1,0:T(8,128)S(1)}, f32[1,256]{1,0:T(1,128)S(1)}, f32[1,256]{1,0:T(1,128)S(1)}) custom-call(s32[1]{0:T(128)} %bitcast.core_ref, bf16[16,2,32,256]{3,2,1,0:T(8,128)(2,1)S(1)} %bitcast.7, bf16[16,32,256]{2,1,0:T(8,128)(2,1)S(1)} %all_to_all.15.own_ref, bf16[16,32,256]{2,1,0:T(8,128)(2,1)S(1)} %collective-permute-done.other_ref, ...), custom_call_target="tpu_custom_call" | custom-call | flops 300000000 | bytes 2097152 | tf_op jit(solution)/shard_map/pallas_call | solution.py:90
  52.3 5.7 %collective-permute-start.1 = (f32[1,256]{1,0:T(1,128)S(1)}, f32[1,256]{1,0:T(1,128)S(1)}, u32[]{:S(2)}, u32[]{:S(2)}) collective-permute-start(f32[1,256]{1,0:T(1,128)S(1)} %broadcast_select_fusion), channel_id=1, source_target_pairs={{0,16},{16,0},{32,48},{48,32},{64,80},{80,64},{96,112},{112,96},{1... | collective-permute-start | bytes 3080 | tf_op jit(solution)/shard_map/ppermute | solution.py:104
  58.1 0.8 collective-permute-done.1
  58.9 10.7 %all_to_all.16 = f32[16,2,256]{2,1,0:T(2,128)S(1)} all-to-all(f32[16,2,256]{2,1,0:T(2,128)S(1)} %broadcast_in_dim.11), channel_id=1, replica_groups={{0,1,2,3,4,5,6,7,8,9,10,11,12,13,14,15},{32,33,34,35,36,37,38,39,40,41,..., dimensions={0} | all-to-all | bytes 65536 | tf_op jit(solution)/shard_map/all_to_all | solution.py:110
  69.7 8.6 %collective-permute-start.2 = (f32[256]{0:T(256)S(1)}, f32[256]{0:T(256)S(1)}, u32[]{:S(2)}, u32[]{:S(2)}) collective-permute-start(f32[256]{0:T(256)S(1)} %bitcast.12), channel_id=1, source_target_pairs={{0,16},{16,0},{32,48},{48,32},{64,80},{80,64},{96,112},{112,96},{1... | collective-permute-start | bytes 3080 | tf_op jit(solution)/shard_map/ppermute | solution.py:113
  78.3 0.8 collective-permute-done.2
  79.1 0.0 copy-start.3
  79.1 0.0 copy-start.4
  79.1 0.6 copy-done.3
  79.6 0.0 copy-done.4
  79.6 0.8 divide_convert_fusion
  (12 shorter events, 0.1 us)
Async XLA Ops:
  1.4 19.7 %copy-start = (bf16[256,64]{0,1:T(8,128)(2,1)S(1)}, bf16[256,64]{0,1:T(8,128)(2,1)}, u32[]{:S(2)}) copy-start(bf16[256,64]{0,1:T(8,128)(2,1)} %param.4) | copy-start | bytes 98308
  21.9 12.8 %copy-start.1 = (s32[256,16]{0,1:T(8,128)S(1)}, s32[256,16]{0,1:T(8,128)}, u32[]{:S(2)}) copy-start(s32[256,16]{0,1:T(8,128)} %param.6) | copy-start | bytes 49156
  21.9 29.2 %all-to-all-start.1 = ((bf16[16,64,256]{2,1,0:T(8,128)(2,1)}), bf16[16,64,256]{2,1,0:T(8,128)(2,1)S(1)}, u32[]{:S(2)}, u32[]{:S(2)}) async-start(bf16[16,64,256]{2,1,0:T(8,128)(2,1)} %broadcast_in_dim.9), calls=%async_computation.1 | async-start | bytes 1048576 | tf_op jit(solution)/shard_map/all_to_all | solution.py:86
  34.8 5.5 %collective-permute-start = (bf16[16,32,256]{2,1,0:T(8,128)(2,1)S(1)}, bf16[16,32,256]{2,1,0:T(8,128)(2,1)S(1)}, u32[]{:S(2)}, u32[]{:S(2)}) collective-permute-start(bf16[16,32,256]{2,1,0:T(8,128)(2,1)S(1)} %all_to_all.15.own_ref), channel_id=1, source_target_pairs={{0,16},{16,0},{32,48},{48,32},{64,80},{80,64},{96,112},{112,96},{1... | collective-permute-start | bytes 786440 | tf_op jit(solution)/shard_map/ppermute | solution.py:85
  39.2 0.7 copy-start.2
  52.3 6.6 %collective-permute-start.1 = (f32[1,256]{1,0:T(1,128)S(1)}, f32[1,256]{1,0:T(1,128)S(1)}, u32[]{:S(2)}, u32[]{:S(2)}) collective-permute-start(f32[1,256]{1,0:T(1,128)S(1)} %broadcast_select_fusion), channel_id=1, source_target_pairs={{0,16},{16,0},{32,48},{48,32},{64,80},{80,64},{96,112},{112,96},{1... | collective-permute-start | bytes 3080 | tf_op jit(solution)/shard_map/ppermute | solution.py:104
  69.7 9.4 %collective-permute-start.2 = (f32[256]{0:T(256)S(1)}, f32[256]{0:T(256)S(1)}, u32[]{:S(2)}, u32[]{:S(2)}) collective-permute-start(f32[256]{0:T(256)S(1)} %bitcast.12), channel_id=1, source_target_pairs={{0,16},{16,0},{32,48},{48,32},{64,80},{80,64},{96,112},{112,96},{1... | collective-permute-start | bytes 3080 | tf_op jit(solution)/shard_map/ppermute | solution.py:113
  79.1 0.6 copy-start.3
  79.1 0.6 copy-start.4

commit v2 on v1

v2 whole, which is shorter than its diff:
```python
import itertools

import jax
import jax.numpy as jnp
from jax import lax
from jax.experimental import pallas as pl
from jax.experimental.pallas import tpu as pltpu
from jax.sharding import PartitionSpec as P

EPSILON = 1e-06
LANES = 128
CORES = 2
ROW = 4
MAJOR = (((0,), (0,)), ((), ()))


def spread(values, count):
    return jnp.broadcast_to(values[None], (count,) + values.shape)


def inverse_norms(values):
    wide = values.astype(jnp.float32)
    return lax.rsqrt(jnp.sum(wide * wide, axis=0, keepdims=True) + EPSILON)


def picked(cosines, index):
    total = jnp.zeros(index.shape, jnp.float32)
    for half in range(cosines.shape[1] // LANES):
        block = cosines[:, half * LANES : (half + 1) * LANES]
        found = jnp.take_along_axis(block, index & (LANES - 1), axis=1)
        total = total + jnp.where(index >> 7 == half, found, 0.0)
    return jnp.sum(total.T, axis=0, keepdims=True)


def lanes_of(near, start):
    count, rows = near.shape
    fill = jnp.full((LANES - count, rows), -1, jnp.int32)
    return jnp.concatenate([near - start, fill], axis=0).T


def target_kernel(start_ref, t_ref, near_t_ref, near_s_ref, ordered_ref, scale_ref, lanes_t_ref, lanes_s_ref):
    cores, fars, planes, closes = t_ref.shape[:4]
    order = itertools.product(range(planes), range(fars), range(closes), range(cores))
    targets = jnp.concatenate([t_ref[c, far, p, close] for p, far, close, c in order], axis=0)
    ordered_ref[...] = targets
    scale_ref[...] = inverse_norms(targets)
    lanes_t_ref[...] = lanes_of(near_t_ref[...], start_ref[0])
    lanes_s_ref[...] = lanes_of(near_s_ref[...], start_ref[1])


def tile_kernel(s_ref, t_ref, scale_ref, lanes_t_ref, lanes_s_ref, cos_ref, row_ref, col_ref):
    sources = s_ref[...]
    targets = t_ref[...]
    s_scale = inverse_norms(sources)
    t_scale = scale_ref[...]

    def product(a, b):
        return lax.dot_general(a, b, MAJOR, preferred_element_type=jnp.float32)

    def column(scale):
        return jnp.broadcast_to(scale, (8, scale.shape[1])).T[:, :1]

    cosines = product(sources, targets) * column(s_scale) * t_scale
    cos_ref[...] = cosines
    row_ref[...] = picked(cosines, lanes_t_ref[...])
    flipped = product(targets, sources) * column(t_scale) * s_scale
    col_ref[...] = picked(flipped, lanes_s_ref[...])


def local(src_embed, tgt_embed, src_near, tgt_near):
    src_index = lax.axis_index("src")
    tgt_index = lax.axis_index("tgt")
    core = src_index % CORES
    src_size = lax.axis_size("src")
    tgt_size = lax.axis_size("tgt")
    chips = src_size // CORES
    src_count, near_count = src_near.shape
    tgt_count = tgt_near.shape[0]
    pairs = [[q * CORES + c for c in range(CORES)] for q in range(chips)]
    near_line = ROW // 2
    planes = chips // ROW

    def device(plane, far, close, c):
        return ((plane * 2 + far) * near_line + close) * CORES + c

    blocks = [
        [device(p, far, close, c) for p in range(planes) for close in range(near_line)]
        for far in range(2)
        for c in range(CORES)
    ]
    far_pairs = [
        [device(p, far, close, c) for far in range(2)]
        for p in range(planes)
        for close in range(near_line)
        for c in range(CORES)
    ]

    def index_of(s, t):
        return s * tgt_size + t

    lines = [[index_of(q * CORES, t) for t in range(tgt_size)] for q in range(chips)]
    lines += [[index_of(q * CORES + 1, t) for q in range(chips)] for t in range(tgt_size)]

    starts = jnp.stack([tgt_index * tgt_count, src_index * src_count]).astype(jnp.int32)
    own = lax.all_to_all(spread(tgt_embed.T, len(blocks[0])), "src", 0, 0, axis_index_groups=blocks)
    own, src_part = lax.optimization_barrier((own, src_embed))
    source = lax.all_to_all(spread(src_part.T, tgt_size), "tgt", 0, 0)
    source = source.reshape(-1, src_count)
    own = own.reshape(planes, near_line, -1, tgt_count)
    halves = lax.all_gather(own, "src", axis=0, axis_index_groups=far_pairs)
    halves = lax.all_gather(halves, "src", axis=0, axis_index_groups=pairs)
    smem = pl.BlockSpec(memory_space=pltpu.SMEM)
    vmem = pl.BlockSpec(memory_space=pltpu.VMEM)
    wide = (src_count, LANES)
    targets, scale, lanes_t, lanes_s = pl.pallas_call(
        target_kernel,
        in_specs=[smem] + [vmem] * 3,
        out_specs=[vmem] * 4,
        out_shape=[
            jax.ShapeDtypeStruct((source.shape[0], tgt_count), jnp.bfloat16),
            jax.ShapeDtypeStruct((1, tgt_count), jnp.float32),
            jax.ShapeDtypeStruct(wide, jnp.int32),
            jax.ShapeDtypeStruct((tgt_count, LANES), jnp.int32),
        ],
        compiler_params=pltpu.CompilerParams(vmem_limit_bytes=32 * 1024 * 1024),
        cost_estimate=pl.CostEstimate(flops=1_000_000, bytes_accessed=2**20, transcendentals=256),
    )(starts, halves, src_near.T, tgt_near.T)
    cosines, row, col = pl.pallas_call(
        tile_kernel,
        in_specs=[vmem] * 5,
        out_specs=[vmem] * 3,
        out_shape=[
            jax.ShapeDtypeStruct((src_count, tgt_count), jnp.float32),
            jax.ShapeDtypeStruct((1, src_count), jnp.float32),
            jax.ShapeDtypeStruct((1, tgt_count), jnp.float32),
        ],
        compiler_params=pltpu.CompilerParams(vmem_limit_bytes=32 * 1024 * 1024),
        cost_estimate=pl.CostEstimate(flops=300_000_000, bytes_accessed=2**21, transcendentals=512),
    )(source, targets, scale, lanes_t, lanes_s)

    first = core == 0
    both = lax.all_gather(
        jnp.concatenate([row, col], axis=0), "src", axis=0, axis_index_groups=pairs
    )
    sums = jnp.where(first, both[:, 0], jnp.broadcast_to(jnp.sum(both[:, 1], axis=0), (2, tgt_count)))
    parts = lax.all_to_all(spread(sums, chips), ("src", "tgt"), 0, 0, axis_index_groups=lines)
    averages = jnp.sum(parts, axis=0) / near_count
    both = lax.all_gather(averages, "src", axis=0, axis_index_groups=pairs)
    src_average = jnp.where(first, both[0, 0], both[0, 1])
    tgt_average = both[1, 0]
    margin = (cosines / ((src_average[:, None] + tgt_average[None, :]) / 2.0)).astype(
        jnp.bfloat16
    )
    return (margin, src_average, tgt_average)


def solution(mesh):
    placed = (P("src", "tgt"), P("tgt", "src"), P("src", None), P("tgt", None))
    return jax.shard_map(
        local,
        mesh=mesh,
        in_specs=placed,
        out_specs=(P("src", "tgt"), P("src"), P("tgt")),
        check_vma=False,
    )
```

time: 81 us -> 73.3 us (0.905)
  blocking collectives: 30.4 us -> 50.4 us
  starting transfers between devices: 31.5 us -> 12.7 us
  waiting for transfers between devices: 12.6 us -> 4.01 us
  local copies, waits for them, and re-layouts: 3.1 us -> 2.15 us
    all_gather x0 -> x4, blocking collectives: none -> 24.7 us  [the longest x1 8.15 us: local(): both = lax.all_gather(averages, 'src', axis=0, axis_index_groups=pairs)]
    ppermute x3 -> x0, starting transfers between devices: 18.7 us -> none  [the longest x1 8.6 us: local(): crossed = lax.ppermute(averages[1], 'src', pair)]
    all_to_all x1, waiting for transfers between devices: 10.8 us -> 4.01 us  [local(): source = lax.all_to_all(spread(src_part.T, tgt_size), 'tgt', 0, 0)]
    all_to_all x1, blocking collectives: 19.7 us -> 14.8 us  [local(): lax.all_to_all(spread(tgt_embed.T, len(blocks[0])), 'src', 0, 0, axis_ind...]
    ppermute x3 -> x0, waiting for transfers between devices: 1.82 us -> none  [the longest x1 0.8 us: local(): crossed = lax.ppermute(averages[1], 'src', pair)]
    unnamed x12 -> x10, local copies, waits for them, and re-layouts: 1.48 us -> 0.58 us
    pallas_call x1 -> x2, Pallas kernels: 1.18 us -> 1.94 us  [the longest x1 1.17 us: local(): pl.pallas_call(tile_kernel, in_specs=[vmem] * 5, out_specs=[vmem] * 3, ou...]
  transfers between devices with their start and end apart: 4 -> 1, of which waited for: 4 -> 1; matrix products, arithmetic and copies ran while one was open for 0% -> 0% of each run, Pallas kernels for 0% -> 1%
where the time goes in v2:
time: 73.3 us; the launch traced here: 72.8 us
  blocking collectives  50.4 us (69%)
  starting transfers between devices  12.7 us (17%)
  waiting for transfers between devices  4.01 us (5%)
  local copies, waits for them, and re-layouts  2.15 us (3%)
  Pallas kernels  1.94 us (3%)
  other arithmetic  0.92 us (1%)
    all_to_all x1, blocking collectives, local(): lax.all_to_all(spread(tgt_embed.T, len(blocks[0])), 'src', 0, 0, axis_ind...  14.8 us
    all_to_all x1, starting transfers between devices, local(): source = lax.all_to_all(spread(src_part.T, tgt_size), 'tgt', 0, 0)  12.7 us
    all_to_all x1, blocking collectives, local(): lax.all_to_all(spread(sums, chips), ('src', 'tgt'), 0, 0, axis_index_grou...  11 us
    all_gather x1, blocking collectives, local(): both = lax.all_gather(averages, 'src', axis=0, axis_index_groups=pairs)  8.15 us
    all_gather x1, blocking collectives, local(): halves = lax.all_gather(own, 'src', axis=0, axis_index_groups=far_pairs)  5.99 us
    all_gather x1, blocking collectives, local(): halves = lax.all_gather(halves, 'src', axis=0, axis_index_groups=pairs)  5.44 us
    all_gather x1, blocking collectives, local(): lax.all_gather(jnp.concatenate([row, col], axis=0), 'src', axis=0, axis_i...  5.12 us
    all_to_all x1, waiting for transfers between devices, local(): source = lax.all_to_all(spread(src_part.T, tgt_size), 'tgt', 0, 0)  4.01 us
  transfers between devices with their start and end apart: 1, of which 1 were waited for; matrix products, arithmetic and copies ran while one was open for 0% of the time, Pallas kernels for 1%

profile of v2, /device:TPU:1, one launch (start us, length us, event | category | flops | bytes accessed | tf_op | source)
XLA Modules:
  0.0 72.8 jit_solution(7142447155051482924)
XLA Ops:
  0.6 0.7 broadcast_in_dim.8
  1.4 0.0 copy-start.2
  1.4 14.8 %all_to_all.15 = bf16[8,32,256]{2,1,0:T(8,128)(2,1)S(1)} all-to-all(bf16[8,32,256]{2,1,0:T(8,128)(2,1)S(1)} %broadcast_in_dim.8), channel_id=1, replica_groups={{0,32,128,160,256,288,384,416},{16,48,144,176,272,304,400,432},{64,96,1..., dimensions={0} | all-to-all | bytes 262144 | tf_op jit(solution)/shard_map/all_to_all | solution.py:105
  16.1 0.0 copy-done.2
  16.1 0.8 %broadcast_in_dim.9 = bf16[16,64,256]{2,1,0:T(8,128)(2,1)} broadcast(bf16[64,256]{1,0:T(8,128)(2,1)S(1)} %bitcast.22), dimensions={1,2} | broadcast | bytes 557056 | tf_op jit(solution)/shard_map/broadcast_in_dim | solution.py:18
  17.0 12.7 %all-to-all-start.1 = ((bf16[16,64,256]{2,1,0:T(8,128)(2,1)}), bf16[16,64,256]{2,1,0:T(8,128)(2,1)S(1)}, u32[]{:S(2)}, u32[]{:S(2)}) async-start(bf16[16,64,256]{2,1,0:T(8,128)(2,1)} %broadcast_in_dim.9), calls=%async_computation.1 | async-start | bytes 1048576 | tf_op jit(solution)/shard_map/all_to_all | solution.py:107
  29.7 0.1 pad_add_fusion.start_ref
  29.7 6.0 %all_gather.19 = bf16[2,4,2,32,256]{4,3,2,1,0:T(8,128)(2,1)S(1)} all-gather(bf16[1,4,2,32,256]{4,3,2,1,0:T(8,128)(2,1)S(1)} %bitcast.21), channel_id=1, replica_groups={{0,64},{16,80},{32,96},{48,112},{128,192},{144,208},{160,224},{176,240}..., dimensions={0}, use_global_device_ids=true | all-gather | bytes 393216 | tf_op jit(solution)/shard_map/all_gather | solution.py:110
  35.7 0.0 copy-start
  35.7 0.0 copy-start.1
  35.7 5.4 %all-gather = bf16[4,4,2,32,256]{4,3,2,1,0:T(8,128)(2,1)S(1)} all-gather(bf16[2,4,2,32,256]{4,3,2,1,0:T(8,128)(2,1)S(1)} %all_gather.19), channel_id=2, replica_groups={{0,16},{32,48},{64,80},{96,112},{128,144},{160,176},{192,208},{224,240}..., dimensions={0}, use_global_device_ids=true | all-gather | bytes 786432 | tf_op jit(solution)/shard_map/all_gather | solution.py:111
  41.2 0.0 copy-done
  41.2 0.0 copy-done.1
  41.2 0.8 %shard_map.67 = (bf16[1024,256]{1,0:T(8,128)(2,1)S(1)}, f32[1,256]{1,0:T(1,128)S(1)}, s32[256,128]{1,0:T(8,128)S(1)}, s32[256,128]{1,0:T(8,128)S(1)}) custom-call(s32[2]{0:T(128)S(1)} %pad_add_fusion.start_ref, bf16[2,2,4,2,32,256]{5,4,3,2,1,0:T(8,128)(2,1)S(1)} %bitcast.17, s32[16,256]{1,0:T(8,128)S(1)} %bitcast.19, s32[16,256]{1,0:T(8,128)S(1)} %bitcast.20), custom_call_target="tpu_custom_call" | custom-call | flops 1000000 | bytes 1048576 | tf_op jit(solution)/shard_map/pallas_call | solution.py:115
  42.0 4.0 %all-to-all-done.1 = bf16[16,64,256]{2,1,0:T(8,128)(2,1)S(1)} async-done(((bf16[16,64,256]{2,1,0:T(8,128)(2,1)}), bf16[16,64,256]{2,1,0:T(8,128)(2,1)S(1)}, u32[]{:S(2)}, u32[]{:S(2)}) %all-to-all-start.1) | async-done | bytes 524320 | tf_op jit(solution)/shard_map/all_to_all | solution.py:107
  46.0 1.2 %shard_map.68 = (f32[256,256]{1,0:T(8,128)S(1)}, f32[1,256]{1,0:T(1,128)S(1)}, f32[1,256]{1,0:T(1,128)S(1)}) custom-call(bf16[1024,256]{1,0:T(8,128)(2,1)S(1)} %bitcast.18, bf16[1024,256]{1,0:T(8,128)(2,1)S(1)} %get-tuple-element.14.t_ref, f32[1,256]{1,0:T(1,128)S(1)} %get-tuple-element.15.scale_ref, s32[256,128]{1,0:T(8,128)S(1)} %get-tuple-element.16.lanes_t_ref, ...), custom_call_target="tpu_custom_call" | custom-call | flops 300000000 | bytes 2097152 | tf_op jit(solution)/shard_map/pallas_call | solution.py:128
  47.2 5.1 %all-gather.3 = f32[2,2,256]{2,1,0:T(2,128)S(1)} all-gather(f32[1,2,256]{2,1,0:T(2,128)S(1)} %maximum_bitcast_fusion), channel_id=3, replica_groups={{0,16},{32,48},{64,80},{96,112},{128,144},{160,176},{192,208},{224,240}..., dimensions={0}, use_global_device_ids=true | all-gather | bytes 6144 | tf_op jit(solution)/shard_map/all_gather | solution.py:142
  52.3 11.0 %all_to_all.16 = f32[16,2,256]{2,1,0:T(2,128)S(1)} all-to-all(f32[16,2,256]{2,1,0:T(2,128)S(1)} %broadcast_in_dim.11), channel_id=1, replica_groups={{0,1,2,3,4,5,6,7,8,9,10,11,12,13,14,15},{32,33,34,35,36,37,38,39,40,41,..., dimensions={0} | all-to-all | bytes 65536 | tf_op jit(solution)/shard_map/all_to_all | solution.py:146
  63.3 8.1 %all-gather.4 = f32[2,2,256]{2,1,0:T(2,128)S(1)} all-gather(f32[1,2,256]{2,1,0:T(2,128)S(1)} %multiply_bitcast_fusion), channel_id=4, replica_groups={{0,16},{32,48},{64,80},{96,112},{128,144},{160,176},{192,208},{224,240}..., dimensions={0}, use_global_device_ids=true | all-gather | bytes 6144 | tf_op jit(solution)/shard_map/all_gather | solution.py:148
  71.5 0.0 copy-start.3
  71.5 0.0 copy-start.4
  71.5 0.6 copy-done.3
  72.1 0.0 copy-done.4
  72.1 0.8 %divide_convert_fusion = bf16[256,256]{1,0:T(8,128)(2,1)} fusion(f32[256,256]{1,0:T(8,128)S(1)} %get-tuple-element.18, f32[256]{0:T(256)S(1)} %bitcast.26, f32[256]{0:T(256)S(1)} %bitcast.24), kind=kLoop, calls=%fused_computation | loop fusion | flops 262144 | bytes 395264 | tf_op jit(solution)/shard_map/convert_element_type | solution.py:151
  (7 shorter events, 0.1 us)
Async XLA Ops:
  1.4 14.8 %copy-start.2 = (bf16[256,64]{0,1:T(8,128)(2,1)S(1)}, bf16[256,64]{0,1:T(8,128)(2,1)}, u32[]{:S(2)}) copy-start(bf16[256,64]{0,1:T(8,128)(2,1)} %param.4) | copy-start | bytes 98308
  17.0 29.0 %all-to-all-start.1 = ((bf16[16,64,256]{2,1,0:T(8,128)(2,1)}), bf16[16,64,256]{2,1,0:T(8,128)(2,1)S(1)}, u32[]{:S(2)}, u32[]{:S(2)}) async-start(bf16[16,64,256]{2,1,0:T(8,128)(2,1)} %broadcast_in_dim.9), calls=%async_computation.1 | async-start | bytes 1048576 | tf_op jit(solution)/shard_map/all_to_all | solution.py:107
  35.7 5.5 %copy-start = (s32[256,16]{0,1:T(8,128)S(1)}, s32[256,16]{0,1:T(8,128)}, u32[]{:S(2)}) copy-start(s32[256,16]{0,1:T(8,128)} %param.6) | copy-start | bytes 49156
  35.7 5.5 %copy-start.1 = (s32[256,16]{0,1:T(8,128)S(1)}, s32[256,16]{0,1:T(8,128)}, u32[]{:S(2)}) copy-start(s32[256,16]{0,1:T(8,128)} %param.7) | copy-start | bytes 49156
  71.5 0.6 copy-start.3
  71.5 0.6 copy-start.4

commit v3 on v2

--- a/solution.py
+++ b/solution.py
@@ -39,9 +39,13 @@
 
 
 def target_kernel(start_ref, t_ref, near_t_ref, near_s_ref, ordered_ref, scale_ref, lanes_t_ref, lanes_s_ref):
-    cores, fars, planes, closes = t_ref.shape[:4]
+    fars, cores, planes, closes = t_ref.shape[:4]
     order = itertools.product(range(planes), range(fars), range(closes), range(cores))
-    targets = jnp.concatenate([t_ref[c, far, p, close] for p, far, close, c in order], axis=0)
+    pieces = [t_ref[far, c, p, close] for p, far, close, c in order]
+    half = len(pieces) // 2
+    targets = jnp.concatenate(
+        [pieces[h * half + k + c] for k in range(0, half, cores) for h in range(2) for c in range(cores)], axis=0
+    )
     ordered_ref[...] = targets
     scale_ref[...] = inverse_norms(targets)
     lanes_t_ref[...] = lanes_of(near_t_ref[...], start_ref[0])
@@ -67,6 +71,16 @@
     col_ref[...] = picked(flipped, lanes_s_ref[...])
 
 
+def margin_kernel(core_ref, both_ref, cos_ref, margin_ref, src_ref, tgt_ref):
+    src_average = both_ref[0, pl.ds(core_ref[0], 1)]
+    tgt_average = both_ref[1, :1]
+    src_ref[...] = src_average
+    tgt_ref[...] = tgt_average
+    rows = src_average.shape[1]
+    column = jnp.broadcast_to(src_average, (8, rows)).T[:, :1]
+    margin_ref[...] = (cos_ref[...] / ((column + tgt_average) / 2.0)).astype(jnp.bfloat16)
+
+
 def local(src_embed, tgt_embed, src_near, tgt_near):
     src_index = lax.axis_index("src")
     tgt_index = lax.axis_index("tgt")
@@ -77,6 +91,9 @@
     src_count, near_count = src_near.shape
     tgt_count = tgt_near.shape[0]
     pairs = [[q * CORES + c for c in range(CORES)] for q in range(chips)]
+    line = tgt_size // 2
+    layers = [[k, k + line] for k in range(line)]
+    lines_y = [[h * line + k for k in range(line)] for h in range(2)]
     near_line = ROW // 2
     planes = chips // ROW
 
@@ -88,11 +105,10 @@
         for far in range(2)
         for c in range(CORES)
     ]
-    far_pairs = [
-        [device(p, far, close, c) for far in range(2)]
+    quads = [
+        [device(p, far, close, c) for far in range(2) for c in range(CORES)]
         for p in range(planes)
         for close in range(near_line)
-        for c in range(CORES)
     ]
 
     def index_of(s, t):
@@ -103,12 +119,13 @@
 
     starts = jnp.stack([tgt_index * tgt_count, src_index * src_count]).astype(jnp.int32)
     own = lax.all_to_all(spread(tgt_embed.T, len(blocks[0])), "src", 0, 0, axis_index_groups=blocks)
-    own, src_part = lax.optimization_barrier((own, src_embed))
-    source = lax.all_to_all(spread(src_part.T, tgt_size), "tgt", 0, 0)
+    src_part = lax.all_gather(src_embed.T, "tgt", axis=0, axis_index_groups=layers)
+    own, src_part = lax.optimization_barrier((own, src_part))
+    source = lax.all_to_all(spread(src_part, line), "tgt", 0, 0, axis_index_groups=lines_y)
     source = source.reshape(-1, src_count)
     own = own.reshape(planes, near_line, -1, tgt_count)
-    halves = lax.all_gather(own, "src", axis=0, axis_index_groups=far_pairs)
-    halves = lax.all_gather(halves, "src", axis=0, axis_index_groups=pairs)
+    halves = lax.all_gather(own, "src", axis=0, axis_index_groups=quads)
+    halves = halves.reshape((2, CORES) + own.shape)
     smem = pl.BlockSpec(memory_space=pltpu.SMEM)
     vmem = pl.BlockSpec(memory_space=pltpu.VMEM)
     wide = (src_count, LANES)
@@ -146,12 +163,19 @@
     parts = lax.all_to_all(spread(sums, chips), ("src", "tgt"), 0, 0, axis_index_groups=lines)
     averages = jnp.sum(parts, axis=0) / near_count
     both = lax.all_gather(averages, "src", axis=0, axis_index_groups=pairs)
-    src_average = jnp.where(first, both[0, 0], both[0, 1])
-    tgt_average = both[1, 0]
-    margin = (cosines / ((src_average[:, None] + tgt_average[None, :]) / 2.0)).astype(
-        jnp.bfloat16
-    )
-    return (margin, src_average, tgt_average)
+    margin, src_average, tgt_average = pl.pallas_call(
+        margin_kernel,
+        in_specs=[smem] + [vmem] * 2,
+        out_specs=[vmem] * 3,
+        out_shape=[
+            jax.ShapeDtypeStruct((src_count, tgt_count), jnp.bfloat16),
+            jax.ShapeDtypeStruct((1, src_count), jnp.float32),
+            jax.ShapeDtypeStruct((1, tgt_count), jnp.float32),
+        ],
+        compiler_params=pltpu.CompilerParams(vmem_limit_bytes=8 * 1024 * 1024),
+        cost_estimate=pl.CostEstimate(flops=200_000, bytes_accessed=2**19, transcendentals=0),
+    )(core.astype(jnp.int32).reshape(1), both, cosines)
+    return (margin, src_average.reshape(src_count), tgt_average.reshape(tgt_count))
 
 
 def solution(mesh):

time: 73.3 us -> 70.7 us (0.965)
  blocking collectives: 50.4 us -> 44.2 us
  starting transfers between devices: 12.7 us -> 15.7 us
  Pallas kernels: 1.94 us -> 2.85 us
  other arithmetic: 0.92 us -> 0.15 us
    all_to_all x1 -> x0, blocking collectives: 14.8 us -> none  [local(): lax.all_to_all(spread(tgt_embed.T, len(blocks[0])), 'src', 0, 0, axis_ind...]
    all_gather x2, blocking collectives: 11.4 us -> 19.3 us  [the longest x1 10.5 us: local(): halves = lax.all_gather(own, 'src', axis=0, axis_index_groups=quads)]
    all_to_all x1 -> x2, starting transfers between devices: 12.7 us -> 15.7 us  [the longest x1 8.87 us: local(): lax.all_to_all(spread(tgt_embed.T, len(blocks[0])), 'src', 0, 0, axis_ind...]
    all_to_all x1, blocking collectives: 11 us -> 13.4 us  [local(): lax.all_to_all(spread(sums, chips), ('src', 'tgt'), 0, 0, axis_index_grou...]
    all_gather x1, blocking collectives: 8.15 us -> 7.2 us  [local(): both = lax.all_gather(averages, 'src', axis=0, axis_index_groups=pairs)]
    pallas_call x0 -> x1, Pallas kernels: none -> 0.92 us  [local(): pl.pallas_call(margin_kernel, in_specs=[smem] + [vmem] * 2, out_specs=[vm...]
    all_gather x1, blocking collectives: 5.12 us -> 4.26 us  [local(): lax.all_gather(jnp.concatenate([row, col], axis=0), 'src', axis=0, axis_i...]
    convert_element_type x1 -> x0, other arithmetic: 0.77 us -> none  [local(): (cosines / ((src_average[:, None] + tgt_average[None, :]) / 2.0)).astype(...]
  transfers between devices with their start and end apart: 1 -> 2, of which waited for: 1 -> 1; matrix products, arithmetic and copies ran while one was open for 0% -> 0% of each run, Pallas kernels for 1% -> 1%
where the time goes in v3:
time: 70.7 us; the launch traced here: 70.2 us
  blocking collectives  44.2 us (63%)
  starting transfers between devices  15.7 us (22%)
  waiting for transfers between devices  4.35 us (6%)
  Pallas kernels  2.85 us (4%)
  local copies, waits for them, and re-layouts  2.24 us (3%)
    all_to_all x1, blocking collectives, local(): lax.all_to_all(spread(sums, chips), ('src', 'tgt'), 0, 0, axis_index_grou...  13.4 us
    all_gather x1, blocking collectives, local(): halves = lax.all_gather(own, 'src', axis=0, axis_index_groups=quads)  10.5 us
    all_to_all x1, starting transfers between devices, local(): lax.all_to_all(spread(tgt_embed.T, len(blocks[0])), 'src', 0, 0, axis_ind...  8.87 us
    all_gather x1, blocking collectives, local(): lax.all_gather(src_embed.T, 'tgt', axis=0, axis_index_groups=layers)  8.87 us
    all_gather x1, blocking collectives, local(): both = lax.all_gather(averages, 'src', axis=0, axis_index_groups=pairs)  7.2 us
    all_to_all x1, starting transfers between devices, local(): lax.all_to_all(spread(src_part, line), 'tgt', 0, 0, axis_index_groups=lin...  6.82 us
    all_to_all x1, waiting for transfers between devices, local(): lax.all_to_all(spread(src_part, line), 'tgt', 0, 0, axis_index_groups=lin...  4.35 us
    all_gather x1, blocking collectives, local(): lax.all_gather(jnp.concatenate([row, col], axis=0), 'src', axis=0, axis_i...  4.26 us
  transfers between devices with their start and end apart: 2, of which 1 were waited for; matrix products, arithmetic and copies ran while one was open for 0% of the time, Pallas kernels for 1%

profile of v3, /device:TPU:1, one launch (start us, length us, event | category | flops | bytes accessed | tf_op | source)
XLA Modules:
  0.0 70.2 jit_solution(2910938966830323870)
XLA Ops:
  0.6 1.4 %broadcast_in_dim.8 = bf16[8,32,256]{2,1,0:T(8,128)(2,1)} broadcast(bf16[32,256]{1,0:T(8,128)(2,1)} %bitcast.26), dimensions={1,2} | broadcast | bytes 147456 | tf_op jit(solution)/shard_map/broadcast_in_dim | solution.py:18
  2.0 0.0 copy-start.2
  2.0 8.9 %all-to-all-start = ((bf16[8,32,256]{2,1,0:T(8,128)(2,1)}), bf16[8,32,256]{2,1,0:T(8,128)(2,1)S(1)}, u32[]{:S(2)}, u32[]{:S(2)}) async-start(bf16[8,32,256]{2,1,0:T(8,128)(2,1)} %broadcast_in_dim.8), calls=%async_computation | async-start | bytes 262144 | tf_op jit(solution)/shard_map/all_to_all | solution.py:121
  10.9 0.0 copy-done.2
  10.9 8.9 %all-gather = bf16[128,256]{1,0:T(8,128)(2,1)S(1)} all-gather(bf16[64,256]{1,0:T(8,128)(2,1)S(1)} %bitcast.25), channel_id=2, replica_groups={{0,8},{1,9},{2,10},{3,11},{4,12},{5,13},{6,14},{7,15},{16,24},{17,25},{..., dimensions={0}, use_global_device_ids=true | all-gather | bytes 98304 | tf_op jit(solution)/shard_map/all_gather | solution.py:122
  19.8 0.0 all-to-all-done
  19.8 0.8 %broadcast_in_dim.9 = bf16[8,2,64,256]{3,2,1,0:T(8,128)(2,1)} broadcast(bf16[2,64,256]{2,1,0:T(8,128)(2,1)S(1)} %bitcast.24), dimensions={1,2,3} | broadcast | bytes 589824 | tf_op jit(solution)/shard_map/broadcast_in_dim | solution.py:18
  20.6 6.8 %all-to-all-start.1 = ((bf16[8,2,64,256]{3,2,1,0:T(8,128)(2,1)}), bf16[8,2,64,256]{3,2,1,0:T(8,128)(2,1)S(1)}, u32[]{:S(2)}, u32[]{:S(2)}) async-start(bf16[8,2,64,256]{3,2,1,0:T(8,128)(2,1)} %broadcast_in_dim.9), calls=%async_computation.1 | async-start | bytes 1048576 | tf_op jit(solution)/shard_map/all_to_all | solution.py:124
  27.4 0.1 pad_add_fusion.start_ref
  27.5 0.0 copy-start
  27.5 0.0 copy-start.1
  27.5 10.5 %all_gather.21 = bf16[4,4,2,32,256]{4,3,2,1,0:T(8,128)(2,1)S(1)} all-gather(bf16[1,4,2,32,256]{4,3,2,1,0:T(8,128)(2,1)S(1)} %bitcast.23), channel_id=1, replica_groups={{0,16,64,80},{32,48,96,112},{128,144,192,208},{160,176,224,240},{256,27..., dimensions={0}, use_global_device_ids=true | all-gather | bytes 655360 | tf_op jit(solution)/shard_map/all_gather | solution.py:127
  38.0 0.0 copy-done
  38.0 0.0 copy-done.1
  38.0 0.8 %shard_map.67 = (bf16[1024,256]{1,0:T(8,128)(2,1)S(1)}, f32[1,256]{1,0:T(1,128)S(1)}, s32[256,128]{1,0:T(8,128)S(1)}, s32[256,128]{1,0:T(8,128)S(1)}) custom-call(s32[2]{0:T(128)S(1)} %pad_add_fusion.start_ref, bf16[2,2,4,2,32,256]{5,4,3,2,1,0:T(8,128)(2,1)S(1)} %bitcast.19, s32[16,256]{1,0:T(8,128)S(1)} %bitcast.21, s32[16,256]{1,0:T(8,128)S(1)} %bitcast.22), custom_call_target="tpu_custom_call" | custom-call | flops 1000000 | bytes 1048576 | tf_op jit(solution)/shard_map/pallas_call | solution.py:132
  38.7 4.3 %all-to-all-done.1 = bf16[8,2,64,256]{3,2,1,0:T(8,128)(2,1)S(1)} async-done(((bf16[8,2,64,256]{3,2,1,0:T(8,128)(2,1)}), bf16[8,2,64,256]{3,2,1,0:T(8,128)(2,1)S(1)}, u32[]{:S(2)}, u32[]{:S(2)}) %all-to-all-start.1) | async-done | bytes 524320 | tf_op jit(solution)/shard_map/all_to_all | solution.py:124
  43.1 1.2 %shard_map.68 = (f32[256,256]{1,0:T(8,128)S(1)}, f32[1,256]{1,0:T(1,128)S(1)}, f32[1,256]{1,0:T(1,128)S(1)}) custom-call(bf16[1024,256]{1,0:T(8,128)(2,1)S(1)} %bitcast.20, bf16[1024,256]{1,0:T(8,128)(2,1)S(1)} %get-tuple-element.17.t_ref, f32[1,256]{1,0:T(1,128)S(1)} %get-tuple-element.18.scale_ref, s32[256,128]{1,0:T(8,128)S(1)} %get-tuple-element.19.lanes_t_ref, ...), custom_call_target="tpu_custom_call" | custom-call | flops 300000000 | bytes 2097152 | tf_op jit(solution)/shard_map/pallas_call | solution.py:145
  44.3 4.3 %all-gather.3 = f32[2,2,256]{2,1,0:T(2,128)S(1)} all-gather(f32[1,2,256]{2,1,0:T(2,128)S(1)} %maximum_bitcast_fusion), channel_id=3, replica_groups={{0,16},{32,48},{64,80},{96,112},{128,144},{160,176},{192,208},{224,240}..., dimensions={0}, use_global_device_ids=true | all-gather | bytes 6144 | tf_op jit(solution)/shard_map/all_gather | solution.py:159
  48.6 13.4 %all_to_all.15 = f32[16,2,256]{2,1,0:T(2,128)S(1)} all-to-all(f32[16,2,256]{2,1,0:T(2,128)S(1)} %broadcast_in_dim.11), channel_id=1, replica_groups={{0,1,2,3,4,5,6,7,8,9,10,11,12,13,14,15},{32,33,34,35,36,37,38,39,40,41,..., dimensions={0} | all-to-all | bytes 65536 | tf_op jit(solution)/shard_map/all_to_all | solution.py:163
  62.0 7.2 %all-gather.4.both_ref = f32[2,2,256]{2,1,0:T(2,128)S(1)} all-gather(f32[1,2,256]{2,1,0:T(2,128)S(1)} %multiply_bitcast_fusion), channel_id=4, replica_groups={{0,16},{32,48},{64,80},{96,112},{128,144},{160,176},{192,208},{224,240}..., dimensions={0}, use_global_device_ids=true | all-gather | bytes 6144 | tf_op jit(solution)/shard_map/all_gather | solution.py:165
  69.2 0.9 %shard_map.69 = (bf16[256,256]{1,0:T(8,128)(2,1)}, f32[1,256]{1,0:T(1,128)}, f32[1,256]{1,0:T(1,128)}) custom-call(s32[1]{0:T(128)} %bitcast.core_ref, f32[2,2,256]{2,1,0:T(2,128)S(1)} %all-gather.4.both_ref, f32[256,256]{1,0:T(8,128)S(1)} %get-tuple-element.23.cos_ref), custom_call_target="tpu_custom_call" | custom-call | flops 200000 | bytes 524288 | tf_op jit(solution)/shard_map/pallas_call | solution.py:166
  (6 shorter events, 0.1 us)
Async XLA Ops:
  2.0 8.9 %copy-start.2 = (bf16[256,64]{0,1:T(8,128)(2,1)S(1)}, bf16[256,64]{0,1:T(8,128)(2,1)}, u32[]{:S(2)}) copy-start(bf16[256,64]{0,1:T(8,128)(2,1)} %param.4) | copy-start | bytes 98308
  2.0 17.7 %all-to-all-start = ((bf16[8,32,256]{2,1,0:T(8,128)(2,1)}), bf16[8,32,256]{2,1,0:T(8,128)(2,1)S(1)}, u32[]{:S(2)}, u32[]{:S(2)}) async-start(bf16[8,32,256]{2,1,0:T(8,128)(2,1)} %broadcast_in_dim.8), calls=%async_computation | async-start | bytes 262144 | tf_op jit(solution)/shard_map/all_to_all | solution.py:121
  20.6 22.5 %all-to-all-start.1 = ((bf16[8,2,64,256]{3,2,1,0:T(8,128)(2,1)}), bf16[8,2,64,256]{3,2,1,0:T(8,128)(2,1)S(1)}, u32[]{:S(2)}, u32[]{:S(2)}) async-start(bf16[8,2,64,256]{3,2,1,0:T(8,128)(2,1)} %broadcast_in_dim.9), calls=%async_computation.1 | async-start | bytes 1048576 | tf_op jit(solution)/shard_map/all_to_all | solution.py:124
  27.5 10.5 %copy-start = (s32[256,16]{0,1:T(8,128)S(1)}, s32[256,16]{0,1:T(8,128)}, u32[]{:S(2)}) copy-start(s32[256,16]{0,1:T(8,128)} %param.6) | copy-start | bytes 49156
  27.5 10.5 %copy-start.1 = (s32[256,16]{0,1:T(8,128)S(1)}, s32[256,16]{0,1:T(8,128)}, u32[]{:S(2)}) copy-start(s32[256,16]{0,1:T(8,128)} %param.7) | copy-start | bytes 49156

commit v4 on v3

--- a/solution.py
+++ b/solution.py
@@ -56,19 +56,13 @@
     sources = s_ref[...]
     targets = t_ref[...]
     s_scale = inverse_norms(sources)
-    t_scale = scale_ref[...]
 
-    def product(a, b):
-        return lax.dot_general(a, b, MAJOR, preferred_element_type=jnp.float32)
-
-    def column(scale):
-        return jnp.broadcast_to(scale, (8, scale.shape[1])).T[:, :1]
-
-    cosines = product(sources, targets) * column(s_scale) * t_scale
+    column = jnp.broadcast_to(s_scale, (8, s_scale.shape[1])).T[:, :1]
+    products = lax.dot_general(sources, targets, MAJOR, preferred_element_type=jnp.float32)
+    cosines = products * column * scale_ref[...]
     cos_ref[...] = cosines
     row_ref[...] = picked(cosines, lanes_t_ref[...])
-    flipped = product(targets, sources) * column(t_scale) * s_scale
-    col_ref[...] = picked(flipped, lanes_s_ref[...])
+    col_ref[...] = picked(cosines.T, lanes_s_ref[...])
 
 
 def margin_kernel(core_ref, both_ref, cos_ref, margin_ref, src_ref, tgt_ref):

time: 70.7 us -> 70.5 us (level)
  no operation moved by 1% of the time
where the time goes in v4:
time: 70.5 us; the launch traced here: 70 us
  blocking collectives  44.2 us (63%)
  starting transfers between devices  15.7 us (22%)
  waiting for transfers between devices  4.35 us (6%)
  Pallas kernels  2.74 us (4%)
  local copies, waits for them, and re-layouts  2.24 us (3%)
    all_to_all x1, blocking collectives, local(): lax.all_to_all(spread(sums, chips), ('src', 'tgt'), 0, 0, axis_index_grou...  13.4 us
    all_gather x1, blocking collectives, local(): halves = lax.all_gather(own, 'src', axis=0, axis_index_groups=quads)  10.5 us
    all_to_all x1, starting transfers between devices, local(): lax.all_to_all(spread(tgt_embed.T, len(blocks[0])), 'src', 0, 0, axis_ind...  8.87 us
    all_gather x1, blocking collectives, local(): lax.all_gather(src_embed.T, 'tgt', axis=0, axis_index_groups=layers)  8.87 us
    all_gather x1, blocking collectives, local(): both = lax.all_gather(averages, 'src', axis=0, axis_index_groups=pairs)  7.19 us
    all_to_all x1, starting transfers between devices, local(): lax.all_to_all(spread(src_part, line), 'tgt', 0, 0, axis_index_groups=lin...  6.82 us
    all_to_all x1, waiting for transfers between devices, local(): lax.all_to_all(spread(src_part, line), 'tgt', 0, 0, axis_index_groups=lin...  4.35 us
    all_gather x1, blocking collectives, local(): lax.all_gather(jnp.concatenate([row, col], axis=0), 'src', axis=0, axis_i...  4.26 us
  transfers between devices with their start and end apart: 2, of which 1 were waited for; matrix products, arithmetic and copies ran while one was open for 0% of the time, Pallas kernels for 1%

profile of v4, /device:TPU:1, one launch (start us, length us, event | category | flops | bytes accessed | tf_op | source)
XLA Modules:
  0.0 70.0 jit_solution(8858934725798528846)
XLA Ops:
  0.6 1.4 %broadcast_in_dim.8 = bf16[8,32,256]{2,1,0:T(8,128)(2,1)} broadcast(bf16[32,256]{1,0:T(8,128)(2,1)} %bitcast.26), dimensions={1,2} | broadcast | bytes 147456 | tf_op jit(solution)/shard_map/broadcast_in_dim | solution.py:18
  2.0 0.0 copy-start.2
  2.0 8.9 %all-to-all-start = ((bf16[8,32,256]{2,1,0:T(8,128)(2,1)}), bf16[8,32,256]{2,1,0:T(8,128)(2,1)S(1)}, u32[]{:S(2)}, u32[]{:S(2)}) async-start(bf16[8,32,256]{2,1,0:T(8,128)(2,1)} %broadcast_in_dim.8), calls=%async_computation | async-start | bytes 262144 | tf_op jit(solution)/shard_map/all_to_all | solution.py:115
  10.9 0.0 copy-done.2
  10.9 8.9 %all-gather = bf16[128,256]{1,0:T(8,128)(2,1)S(1)} all-gather(bf16[64,256]{1,0:T(8,128)(2,1)S(1)} %bitcast.25), channel_id=2, replica_groups={{0,8},{1,9},{2,10},{3,11},{4,12},{5,13},{6,14},{7,15},{16,24},{17,25},{..., dimensions={0}, use_global_device_ids=true | all-gather | bytes 98304 | tf_op jit(solution)/shard_map/all_gather | solution.py:116
  19.8 0.0 all-to-all-done
  19.8 0.8 %broadcast_in_dim.9 = bf16[8,2,64,256]{3,2,1,0:T(8,128)(2,1)} broadcast(bf16[2,64,256]{2,1,0:T(8,128)(2,1)S(1)} %bitcast.24), dimensions={1,2,3} | broadcast | bytes 589824 | tf_op jit(solution)/shard_map/broadcast_in_dim | solution.py:18
  20.6 6.8 %all-to-all-start.1 = ((bf16[8,2,64,256]{3,2,1,0:T(8,128)(2,1)}), bf16[8,2,64,256]{3,2,1,0:T(8,128)(2,1)S(1)}, u32[]{:S(2)}, u32[]{:S(2)}) async-start(bf16[8,2,64,256]{3,2,1,0:T(8,128)(2,1)} %broadcast_in_dim.9), calls=%async_computation.1 | async-start | bytes 1048576 | tf_op jit(solution)/shard_map/all_to_all | solution.py:118
  27.4 0.1 pad_add_fusion.start_ref
  27.5 0.0 copy-start
  27.5 0.0 copy-start.1
  27.5 10.5 %all_gather.21 = bf16[4,4,2,32,256]{4,3,2,1,0:T(8,128)(2,1)S(1)} all-gather(bf16[1,4,2,32,256]{4,3,2,1,0:T(8,128)(2,1)S(1)} %bitcast.23), channel_id=1, replica_groups={{0,16,64,80},{32,48,96,112},{128,144,192,208},{160,176,224,240},{256,27..., dimensions={0}, use_global_device_ids=true | all-gather | bytes 655360 | tf_op jit(solution)/shard_map/all_gather | solution.py:121
  38.0 0.0 copy-done
  38.0 0.0 copy-done.1
  38.0 0.8 %shard_map.67 = (bf16[1024,256]{1,0:T(8,128)(2,1)S(1)}, f32[1,256]{1,0:T(1,128)S(1)}, s32[256,128]{1,0:T(8,128)S(1)}, s32[256,128]{1,0:T(8,128)S(1)}) custom-call(s32[2]{0:T(128)S(1)} %pad_add_fusion.start_ref, bf16[2,2,4,2,32,256]{5,4,3,2,1,0:T(8,128)(2,1)S(1)} %bitcast.19, s32[16,256]{1,0:T(8,128)S(1)} %bitcast.21, s32[16,256]{1,0:T(8,128)S(1)} %bitcast.22), custom_call_target="tpu_custom_call" | custom-call | flops 1000000 | bytes 1048576 | tf_op jit(solution)/shard_map/pallas_call | solution.py:126
  38.7 4.3 %all-to-all-done.1 = bf16[8,2,64,256]{3,2,1,0:T(8,128)(2,1)S(1)} async-done(((bf16[8,2,64,256]{3,2,1,0:T(8,128)(2,1)}), bf16[8,2,64,256]{3,2,1,0:T(8,128)(2,1)S(1)}, u32[]{:S(2)}, u32[]{:S(2)}) %all-to-all-start.1) | async-done | bytes 524320 | tf_op jit(solution)/shard_map/all_to_all | solution.py:118
  43.1 1.1 %shard_map.68 = (f32[256,256]{1,0:T(8,128)S(1)}, f32[1,256]{1,0:T(1,128)S(1)}, f32[1,256]{1,0:T(1,128)S(1)}) custom-call(bf16[1024,256]{1,0:T(8,128)(2,1)S(1)} %bitcast.20, bf16[1024,256]{1,0:T(8,128)(2,1)S(1)} %get-tuple-element.17.t_ref, f32[1,256]{1,0:T(1,128)S(1)} %get-tuple-element.18.scale_ref, s32[256,128]{1,0:T(8,128)S(1)} %get-tuple-element.19.lanes_t_ref, ...), custom_call_target="tpu_custom_call" | custom-call | flops 300000000 | bytes 2097152 | tf_op jit(solution)/shard_map/pallas_call | solution.py:139
  44.2 4.3 %all-gather.3 = f32[2,2,256]{2,1,0:T(2,128)S(1)} all-gather(f32[1,2,256]{2,1,0:T(2,128)S(1)} %maximum_bitcast_fusion), channel_id=3, replica_groups={{0,16},{32,48},{64,80},{96,112},{128,144},{160,176},{192,208},{224,240}..., dimensions={0}, use_global_device_ids=true | all-gather | bytes 6144 | tf_op jit(solution)/shard_map/all_gather | solution.py:153
  48.5 13.4 %all_to_all.15 = f32[16,2,256]{2,1,0:T(2,128)S(1)} all-to-all(f32[16,2,256]{2,1,0:T(2,128)S(1)} %broadcast_in_dim.11), channel_id=1, replica_groups={{0,1,2,3,4,5,6,7,8,9,10,11,12,13,14,15},{32,33,34,35,36,37,38,39,40,41,..., dimensions={0} | all-to-all | bytes 65536 | tf_op jit(solution)/shard_map/all_to_all | solution.py:157
  61.9 7.2 %all-gather.4.both_ref = f32[2,2,256]{2,1,0:T(2,128)S(1)} all-gather(f32[1,2,256]{2,1,0:T(2,128)S(1)} %multiply_bitcast_fusion), channel_id=4, replica_groups={{0,16},{32,48},{64,80},{96,112},{128,144},{160,176},{192,208},{224,240}..., dimensions={0}, use_global_device_ids=true | all-gather | bytes 6144 | tf_op jit(solution)/shard_map/all_gather | solution.py:159
  69.1 0.9 %shard_map.69 = (bf16[256,256]{1,0:T(8,128)(2,1)}, f32[1,256]{1,0:T(1,128)}, f32[1,256]{1,0:T(1,128)}) custom-call(s32[1]{0:T(128)} %bitcast.core_ref, f32[2,2,256]{2,1,0:T(2,128)S(1)} %all-gather.4.both_ref, f32[256,256]{1,0:T(8,128)S(1)} %get-tuple-element.23.cos_ref), custom_call_target="tpu_custom_call" | custom-call | flops 200000 | bytes 524288 | tf_op jit(solution)/shard_map/pallas_call | solution.py:160
  (6 shorter events, 0.1 us)
Async XLA Ops:
  2.0 8.9 %copy-start.2 = (bf16[256,64]{0,1:T(8,128)(2,1)S(1)}, bf16[256,64]{0,1:T(8,128)(2,1)}, u32[]{:S(2)}) copy-start(bf16[256,64]{0,1:T(8,128)(2,1)} %param.4) | copy-start | bytes 98308
  2.0 17.7 %all-to-all-start = ((bf16[8,32,256]{2,1,0:T(8,128)(2,1)}), bf16[8,32,256]{2,1,0:T(8,128)(2,1)S(1)}, u32[]{:S(2)}, u32[]{:S(2)}) async-start(bf16[8,32,256]{2,1,0:T(8,128)(2,1)} %broadcast_in_dim.8), calls=%async_computation | async-start | bytes 262144 | tf_op jit(solution)/shard_map/all_to_all | solution.py:115
  20.6 22.5 %all-to-all-start.1 = ((bf16[8,2,64,256]{3,2,1,0:T(8,128)(2,1)}), bf16[8,2,64,256]{3,2,1,0:T(8,128)(2,1)S(1)}, u32[]{:S(2)}, u32[]{:S(2)}) async-start(bf16[8,2,64,256]{3,2,1,0:T(8,128)(2,1)} %broadcast_in_dim.9), calls=%async_computation.1 | async-start | bytes 1048576 | tf_op jit(solution)/shard_map/all_to_all | solution.py:118
  27.5 10.5 %copy-start = (s32[256,16]{0,1:T(8,128)S(1)}, s32[256,16]{0,1:T(8,128)}, u32[]{:S(2)}) copy-start(s32[256,16]{0,1:T(8,128)} %param.6) | copy-start | bytes 49156
  27.5 10.5 %copy-start.1 = (s32[256,16]{0,1:T(8,128)S(1)}, s32[256,16]{0,1:T(8,128)}, u32[]{:S(2)}) copy-start(s32[256,16]{0,1:T(8,128)} %param.7) | copy-start | bytes 49156

commit v5 on v4

--- a/solution.py
+++ b/solution.py
@@ -10,7 +10,6 @@
 EPSILON = 1e-06
 LANES = 128
 CORES = 2
-ROW = 4
 MAJOR = (((0,), (0,)), ((), ()))
 
 
@@ -39,13 +38,10 @@
 
 
 def target_kernel(start_ref, t_ref, near_t_ref, near_s_ref, ordered_ref, scale_ref, lanes_t_ref, lanes_s_ref):
-    fars, cores, planes, closes = t_ref.shape[:4]
-    order = itertools.product(range(planes), range(fars), range(closes), range(cores))
-    pieces = [t_ref[far, c, p, close] for p, far, close, c in order]
-    half = len(pieces) // 2
-    targets = jnp.concatenate(
-        [pieces[h * half + k + c] for k in range(0, half, cores) for h in range(2) for c in range(cores)], axis=0
-    )
+    layer = start_ref[2]
+    order = itertools.product(range(t_ref.shape[2]), range(2), range(t_ref.shape[0]))
+    pieces = [t_ref[c, lax.rem(layer + h, 2), p] for p, h, c in order]
+    targets = jnp.concatenate(pieces, axis=0)
     ordered_ref[...] = targets
     scale_ref[...] = inverse_norms(targets)
     lanes_t_ref[...] = lanes_of(near_t_ref[...], start_ref[0])
@@ -86,24 +82,13 @@
     tgt_count = tgt_near.shape[0]
     pairs = [[q * CORES + c for c in range(CORES)] for q in range(chips)]
     line = tgt_size // 2
-    layers = [[k, k + line] for k in range(line)]
+    layer = tgt_index // line
+    partners = [(k, k ^ line) for k in range(tgt_size)]
     lines_y = [[h * line + k for k in range(line)] for h in range(2)]
-    near_line = ROW // 2
-    planes = chips // ROW
 
-    def device(plane, far, close, c):
-        return ((plane * 2 + far) * near_line + close) * CORES + c
-
-    blocks = [
-        [device(p, far, close, c) for p in range(planes) for close in range(near_line)]
-        for far in range(2)
-        for c in range(CORES)
-    ]
-    quads = [
-        [device(p, far, close, c) for far in range(2) for c in range(CORES)]
-        for p in range(planes)
-        for close in range(near_line)
-    ]
+    half = src_size // 2
+    blocks = [[k * half + q * CORES + c for q in range(chips // 2)] for k in range(2) for c in range(CORES)]
+    far_pairs = [[k, k + half] for k in range(half)]
 
     def index_of(s, t):
         return s * tgt_size + t
@@ -111,15 +96,22 @@
     lines = [[index_of(q * CORES, t) for t in range(tgt_size)] for q in range(chips)]
     lines += [[index_of(q * CORES + 1, t) for q in range(chips)] for t in range(tgt_size)]
 
-    starts = jnp.stack([tgt_index * tgt_count, src_index * src_count]).astype(jnp.int32)
-    own = lax.all_to_all(spread(tgt_embed.T, len(blocks[0])), "src", 0, 0, axis_index_groups=blocks)
-    src_part = lax.all_gather(src_embed.T, "tgt", axis=0, axis_index_groups=layers)
-    own, src_part = lax.optimization_barrier((own, src_part))
-    source = lax.all_to_all(spread(src_part, line), "tgt", 0, 0, axis_index_groups=lines_y)
+    starts = jnp.stack([tgt_index * tgt_count, src_index * src_count, layer]).astype(jnp.int32)
+    mine = src_embed.T
+    partner = lax.ppermute(mine, "tgt", partners)
+    copies = len(blocks[0])
+    own = lax.cond(
+        src_index + tgt_index < src_size + tgt_size,
+        lambda part: lax.all_to_all(spread(part, copies), "src", 0, 0, axis_index_groups=blocks),
+        lambda part: lax.all_gather(part, "src", axis=0, axis_index_groups=blocks),
+        tgt_embed.T,
+    )
+    own, mine, partner = lax.optimization_barrier((own, mine, partner))
+    operand = spread(jnp.stack([mine, partner]), line)
+    source = lax.all_to_all(operand, "tgt", 0, 0, axis_index_groups=lines_y)
     source = source.reshape(-1, src_count)
-    own = own.reshape(planes, near_line, -1, tgt_count)
-    halves = lax.all_gather(own, "src", axis=0, axis_index_groups=quads)
-    halves = halves.reshape((2, CORES) + own.shape)
+    halves = lax.all_gather(own, "src", axis=0, axis_index_groups=far_pairs)
+    halves = lax.all_gather(halves, "src", axis=0, axis_index_groups=pairs)
     smem = pl.BlockSpec(memory_space=pltpu.SMEM)
     vmem = pl.BlockSpec(memory_space=pltpu.VMEM)
     wide = (src_count, LANES)

time: 70.5 us -> 69.2 us (0.982)
  waiting for transfers between devices: 4.35 us -> 1.33 us
  starting transfers between devices: 15.7 us -> 18.3 us
  local copies, waits for them, and re-layouts: 2.24 us -> 0.88 us
    ppermute x0 -> x1, starting transfers between devices: none -> 11.5 us  [local(): partner = lax.ppermute(mine, 'tgt', partners)]
    all_to_all x0 -> x1, blocking collectives: none -> 10.2 us  [local(): lax.all_to_all(spread(part, copies), 'src', 0, 0, axis_index_groups=blocks)]
    all_to_all x2 -> x1, starting transfers between devices: 15.7 us -> 6.82 us  [local(): source = lax.all_to_all(operand, 'tgt', 0, 0, axis_index_groups=lines_y)]
    all_gather x2, blocking collectives: 19.3 us -> 12.5 us  [the longest x1 6.79 us: local(): halves = lax.all_gather(own, 'src', axis=0, axis_index_groups=far_pairs)]
    all_to_all x2 -> x1, waiting for transfers between devices: 4.35 us -> 1.33 us  [local(): source = lax.all_to_all(operand, 'tgt', 0, 0, axis_index_groups=lines_y)]
    all_gather x1, blocking collectives: 7.19 us -> 5.18 us  [local(): both = lax.all_gather(averages, 'src', axis=0, axis_index_groups=pairs)]
    all_to_all x1, blocking collectives: 13.4 us -> 11.6 us  [local(): lax.all_to_all(spread(sums, chips), ('src', 'tgt'), 0, 0, axis_index_grou...]
    broadcast_in_dim x3, local copies, waits for them, and re-layouts: 2.23 us -> 0.87 us  [spread(): return jnp.broadcast_to(values[None], (count,) + values.shape)]
where the time goes in v5:
time: 69.2 us; the launch traced here: 68.8 us
  blocking collectives  44.7 us (65%)
  starting transfers between devices  18.3 us (26%)
  Pallas kernels  2.76 us (4%)
  waiting for transfers between devices  1.33 us (2%)
  local copies, waits for them, and re-layouts  0.88 us (1%)
  between operations  0.7 us (1%)
    all_to_all x1, blocking collectives, local(): lax.all_to_all(spread(sums, chips), ('src', 'tgt'), 0, 0, axis_index_grou...  11.6 us
    ppermute x1, starting transfers between devices, local(): partner = lax.ppermute(mine, 'tgt', partners)  11.5 us
    all_to_all x1, blocking collectives, local(): lax.all_to_all(spread(part, copies), 'src', 0, 0, axis_index_groups=blocks)  10.2 us
    all_to_all x1, starting transfers between devices, local(): source = lax.all_to_all(operand, 'tgt', 0, 0, axis_index_groups=lines_y)  6.82 us
    all_gather x1, blocking collectives, local(): halves = lax.all_gather(own, 'src', axis=0, axis_index_groups=far_pairs)  6.79 us
    all_gather x1, blocking collectives, local(): halves = lax.all_gather(halves, 'src', axis=0, axis_index_groups=pairs)  5.74 us
    all_gather x1, blocking collectives, local(): lax.all_gather(jnp.concatenate([row, col], axis=0), 'src', axis=0, axis_i...  5.2 us
    all_gather x1, blocking collectives, local(): both = lax.all_gather(averages, 'src', axis=0, axis_index_groups=pairs)  5.18 us
  transfers between devices with their start and end apart: 2, of which 1 were waited for; matrix products, arithmetic and copies ran while one was open for 0% of the time, Pallas kernels for 1%

profile of v5, /device:TPU:1, one launch (start us, length us, event | category | flops | bytes accessed | tf_op | source)
XLA Modules:
  0.0 68.8 jit_solution(15758337041159580860)
XLA Ops:
  0.6 0.0 copy-start.2
  0.6 11.5 %collective-permute-start = (bf16[64,256]{1,0:T(8,128)(2,1)}, bf16[64,256]{1,0:T(8,128)(2,1)S(1)}, u32[]{:S(2)}, u32[]{:S(2)}) collective-permute-start(bf16[64,256]{1,0:T(8,128)(2,1)} %bitcast.30), channel_id=1, source_target_pairs={{0,8},{1,9},{2,10},{3,11},{4,12},{5,13},{6,14},{7,15},{8,0},{9,1},... | collective-permute-start | bytes 98312 | tf_op jit(solution)/shard_map/ppermute | solution.py:101
  12.1 0.0 copy-done.2
  12.1 0.0 copy-start.3
  12.1 10.2 %conditional.1 = (bf16[8,32,256]{2,1,0:T(8,128)(2,1)S(1)}) conditional(s32[]{:T(128)} %convert_element_type.3, bf16[32,256]{1,0:T(8,128)(2,1)S(1)} %bitcast.28, bf16[32,256]{1,0:T(8,128)(2,1)S(1)} %bitcast.29), branch_computations={%region_0.1_spmd, %region_1.2_spmd} | conditional | bytes 409608 | solution.py:103
  12.2 10.2 %all_to_all.14 = bf16[8,32,256]{2,1,0:T(8,128)(2,1)S(1)} all-to-all(bf16[8,32,256]{2,1,0:T(8,128)(2,1)S(1)} %broadcast_in_dim.8), channel_id=1, replica_groups={{0,32,64,96,128,160,192,224},{16,48,80,112,144,176,208,240},{256,288,32..., dimensions={0} | all-to-all | bytes 262144 | tf_op jit(solution)/shard_map/cond/branch_1_fun/all_to_all | solution.py:105
  22.3 0.0 collective-permute-done
  22.3 0.0 copy-done.3
  22.3 0.8 %broadcast_in_dim.12 = bf16[8,2,64,256]{3,2,1,0:T(8,128)(2,1)} broadcast(bf16[2,64,256]{2,1,0:T(8,128)(2,1)S(1)} %pad_maximum_fusion), dimensions={1,2,3} | broadcast | bytes 589824 | tf_op jit(solution)/shard_map/broadcast_in_dim | solution.py:17
  23.2 6.8 %all-to-all-start.1 = ((bf16[8,2,64,256]{3,2,1,0:T(8,128)(2,1)}), bf16[8,2,64,256]{3,2,1,0:T(8,128)(2,1)S(1)}, u32[]{:S(2)}, u32[]{:S(2)}) async-start(bf16[8,2,64,256]{3,2,1,0:T(8,128)(2,1)} %broadcast_in_dim.12), calls=%async_computation.1 | async-start | bytes 1048576 | tf_op jit(solution)/shard_map/all_to_all | solution.py:111
  30.0 0.1 pad_add_fusion.start_ref
  30.1 6.8 %all-gather.1 = bf16[16,32,256]{2,1,0:T(8,128)(2,1)S(1)} all-gather(bf16[8,32,256]{2,1,0:T(8,128)(2,1)S(1)} %get-tuple-element.36), channel_id=3, replica_groups={{0,256},{16,272},{32,288},{48,304},{64,320},{80,336},{96,352},{112,368}..., dimensions={0}, use_global_device_ids=true | all-gather | bytes 393216 | tf_op jit(solution)/shard_map/all_gather | solution.py:113
  36.9 0.0 copy-start
  36.9 0.0 copy-start.1
  36.9 5.7 %all-gather.2 = bf16[4,8,32,256]{3,2,1,0:T(8,128)(2,1)S(1)} all-gather(bf16[2,8,32,256]{3,2,1,0:T(8,128)(2,1)S(1)} %bitcast.26), channel_id=4, replica_groups={{0,16},{32,48},{64,80},{96,112},{128,144},{160,176},{192,208},{224,240}..., dimensions={0}, use_global_device_ids=true | all-gather | bytes 786432 | tf_op jit(solution)/shard_map/all_gather | solution.py:114
  42.6 0.0 copy-done
  42.6 0.0 copy-done.1
  42.6 0.8 %shard_map.67 = (bf16[1024,256]{1,0:T(8,128)(2,1)S(1)}, f32[1,256]{1,0:T(1,128)S(1)}, s32[256,128]{1,0:T(8,128)S(1)}, s32[256,128]{1,0:T(8,128)S(1)}) custom-call(s32[3]{0:T(128)S(1)} %pad_add_fusion.start_ref, bf16[2,2,8,32,256]{4,3,2,1,0:T(8,128)(2,1)S(1)} %bitcast.22, s32[16,256]{1,0:T(8,128)S(1)} %bitcast.24, s32[16,256]{1,0:T(8,128)S(1)} %bitcast.25), custom_call_target="tpu_custom_call" | custom-call | flops 1000000 | bytes 1048576 | tf_op jit(solution)/shard_map/pallas_call | solution.py:118
  43.4 1.3 %all-to-all-done.1 = bf16[8,2,64,256]{3,2,1,0:T(8,128)(2,1)S(1)} async-done(((bf16[8,2,64,256]{3,2,1,0:T(8,128)(2,1)}), bf16[8,2,64,256]{3,2,1,0:T(8,128)(2,1)S(1)}, u32[]{:S(2)}, u32[]{:S(2)}) %all-to-all-start.1) | async-done | bytes 524320 | tf_op jit(solution)/shard_map/all_to_all | solution.py:111
  44.7 1.1 %shard_map.68 = (f32[256,256]{1,0:T(8,128)S(1)}, f32[1,256]{1,0:T(1,128)S(1)}, f32[1,256]{1,0:T(1,128)S(1)}) custom-call(bf16[1024,256]{1,0:T(8,128)(2,1)S(1)} %bitcast.23, bf16[1024,256]{1,0:T(8,128)(2,1)S(1)} %get-tuple-element.24.t_ref, f32[1,256]{1,0:T(1,128)S(1)} %get-tuple-element.25.scale_ref, s32[256,128]{1,0:T(8,128)S(1)} %get-tuple-element.26.lanes_t_ref, ...), custom_call_target="tpu_custom_call" | custom-call | flops 300000000 | bytes 2097152 | tf_op jit(solution)/shard_map/pallas_call | solution.py:131
  45.8 5.2 %all-gather.5 = f32[2,2,256]{2,1,0:T(2,128)S(1)} all-gather(f32[1,2,256]{2,1,0:T(2,128)S(1)} %maximum_bitcast_fusion), channel_id=5, replica_groups={{0,16},{32,48},{64,80},{96,112},{128,144},{160,176},{192,208},{224,240}..., dimensions={0}, use_global_device_ids=true | all-gather | bytes 6144 | tf_op jit(solution)/shard_map/all_gather | solution.py:145
  51.1 11.6 %all_to_all.15 = f32[16,2,256]{2,1,0:T(2,128)S(1)} all-to-all(f32[16,2,256]{2,1,0:T(2,128)S(1)} %broadcast_in_dim.14), channel_id=1, replica_groups={{0,1,2,3,4,5,6,7,8,9,10,11,12,13,14,15},{32,33,34,35,36,37,38,39,40,41,..., dimensions={0} | all-to-all | bytes 65536 | tf_op jit(solution)/shard_map/all_to_all | solution.py:149
  62.7 5.2 %all-gather.6.both_ref = f32[2,2,256]{2,1,0:T(2,128)S(1)} all-gather(f32[1,2,256]{2,1,0:T(2,128)S(1)} %multiply_bitcast_fusion), channel_id=6, replica_groups={{0,16},{32,48},{64,80},{96,112},{128,144},{160,176},{192,208},{224,240}..., dimensions={0}, use_global_device_ids=true | all-gather | bytes 6144 | tf_op jit(solution)/shard_map/all_gather | solution.py:151
  67.9 0.9 %shard_map.69 = (bf16[256,256]{1,0:T(8,128)(2,1)}, f32[1,256]{1,0:T(1,128)}, f32[1,256]{1,0:T(1,128)}) custom-call(s32[1]{0:T(128)} %bitcast.1.core_ref, f32[2,2,256]{2,1,0:T(2,128)S(1)} %all-gather.6.both_ref, f32[256,256]{1,0:T(8,128)S(1)} %get-tuple-element.30.cos_ref), custom_call_target="tpu_custom_call" | custom-call | flops 200000 | bytes 524288 | tf_op jit(solution)/shard_map/pallas_call | solution.py:152
  (8 shorter events, 0.1 us)
Async XLA Ops:
  0.6 11.5 %copy-start.2 = (bf16[256,32]{0,1:T(8,128)(2,1)S(1)}, bf16[256,32]{0,1:T(8,128)(2,1)}, u32[]{:S(2)}) copy-start(bf16[256,32]{0,1:T(8,128)(2,1)} %param.7) | copy-start | bytes 49156
  0.6 21.7 %collective-permute-start = (bf16[64,256]{1,0:T(8,128)(2,1)}, bf16[64,256]{1,0:T(8,128)(2,1)S(1)}, u32[]{:S(2)}, u32[]{:S(2)}) collective-permute-start(bf16[64,256]{1,0:T(8,128)(2,1)} %bitcast.30), channel_id=1, source_target_pairs={{0,8},{1,9},{2,10},{3,11},{4,12},{5,13},{6,14},{7,15},{8,0},{9,1},... | collective-permute-start | bytes 98312 | tf_op jit(solution)/shard_map/ppermute | solution.py:101
  12.1 10.2 %copy-start.3 = (bf16[256,64]{0,1:T(8,128)(2,1)S(1)}, bf16[256,64]{0,1:T(8,128)(2,1)}, u32[]{:S(2)}) copy-start(bf16[256,64]{0,1:T(8,128)(2,1)} %param.6) | copy-start | bytes 98308
  23.2 21.5 %all-to-all-start.1 = ((bf16[8,2,64,256]{3,2,1,0:T(8,128)(2,1)}), bf16[8,2,64,256]{3,2,1,0:T(8,128)(2,1)S(1)}, u32[]{:S(2)}, u32[]{:S(2)}) async-start(bf16[8,2,64,256]{3,2,1,0:T(8,128)(2,1)} %broadcast_in_dim.12), calls=%async_computation.1 | async-start | bytes 1048576 | tf_op jit(solution)/shard_map/all_to_all | solution.py:111
  36.9 5.7 %copy-start = (s32[256,16]{0,1:T(8,128)S(1)}, s32[256,16]{0,1:T(8,128)}, u32[]{:S(2)}) copy-start(s32[256,16]{0,1:T(8,128)} %param.8) | copy-start | bytes 49156
  36.9 5.7 %copy-start.1 = (s32[256,16]{0,1:T(8,128)S(1)}, s32[256,16]{0,1:T(8,128)}, u32[]{:S(2)}) copy-start(s32[256,16]{0,1:T(8,128)} %param.9) | copy-start | bytes 49156

commit v6 on v5

--- a/solution.py
+++ b/solution.py
@@ -62,8 +62,8 @@
 
 
 def margin_kernel(core_ref, both_ref, cos_ref, margin_ref, src_ref, tgt_ref):
-    src_average = both_ref[0, pl.ds(core_ref[0], 1)]
-    tgt_average = both_ref[1, :1]
+    src_average = both_ref[1, pl.ds(core_ref[0], 1)]
+    tgt_average = both_ref[0, :1]
     src_ref[...] = src_average
     tgt_ref[...] = tgt_average
     rows = src_average.shape[1]
@@ -93,8 +93,8 @@
     def index_of(s, t):
         return s * tgt_size + t
 
-    lines = [[index_of(q * CORES, t) for t in range(tgt_size)] for q in range(chips)]
-    lines += [[index_of(q * CORES + 1, t) for q in range(chips)] for t in range(tgt_size)]
+    lines = [[index_of(q * CORES + 1, t) for t in range(tgt_size)] for q in range(chips)]
+    lines += [[index_of(q * CORES, t) for q in range(chips)] for t in range(tgt_size)]
 
     starts = jnp.stack([tgt_index * tgt_count, src_index * src_count, layer]).astype(jnp.int32)
     mine = src_embed.T
@@ -141,11 +141,11 @@
         cost_estimate=pl.CostEstimate(flops=300_000_000, bytes_accessed=2**21, transcendentals=512),
     )(source, targets, scale, lanes_t, lanes_s)
 
-    first = core == 0
+    by_rows = core == 1
     both = lax.all_gather(
         jnp.concatenate([row, col], axis=0), "src", axis=0, axis_index_groups=pairs
     )
-    sums = jnp.where(first, both[:, 0], jnp.broadcast_to(jnp.sum(both[:, 1], axis=0), (2, tgt_count)))
+    sums = jnp.where(by_rows, both[:, 0], jnp.broadcast_to(jnp.sum(both[:, 1], axis=0), (2, tgt_count)))
     parts = lax.all_to_all(spread(sums, chips), ("src", "tgt"), 0, 0, axis_index_groups=lines)
     averages = jnp.sum(parts, axis=0) / near_count
     both = lax.all_gather(averages, "src", axis=0, axis_index_groups=pairs)

time: 69.2 us -> 68.1 us (0.984)
  blocking collectives: 44.7 us -> 43.5 us
    all_gather x1, blocking collectives: 5.18 us -> 1.78 us  [local(): both = lax.all_gather(averages, 'src', axis=0, axis_index_groups=pairs)]
    all_to_all x1, blocking collectives: 11.6 us -> 13.8 us  [local(): lax.all_to_all(spread(sums, chips), ('src', 'tgt'), 0, 0, axis_index_grou...]
where the time goes in v6:
time: 68.1 us; the launch traced here: 67.6 us
  blocking collectives  43.5 us (64%)
  starting transfers between devices  18.3 us (27%)
  Pallas kernels  2.76 us (4%)
  waiting for transfers between devices  1.33 us (2%)
  local copies, waits for them, and re-layouts  0.88 us (1%)
  between operations  0.7 us (1%)
    all_to_all x1, blocking collectives, local(): lax.all_to_all(spread(sums, chips), ('src', 'tgt'), 0, 0, axis_index_grou...  13.8 us
    ppermute x1, starting transfers between devices, local(): partner = lax.ppermute(mine, 'tgt', partners)  11.5 us
    all_to_all x1, blocking collectives, local(): lax.all_to_all(spread(part, copies), 'src', 0, 0, axis_index_groups=blocks)  10.2 us
    all_to_all x1, starting transfers between devices, local(): source = lax.all_to_all(operand, 'tgt', 0, 0, axis_index_groups=lines_y)  6.82 us
    all_gather x1, blocking collectives, local(): halves = lax.all_gather(own, 'src', axis=0, axis_index_groups=far_pairs)  6.79 us
    all_gather x1, blocking collectives, local(): halves = lax.all_gather(halves, 'src', axis=0, axis_index_groups=pairs)  5.74 us
    all_gather x1, blocking collectives, local(): lax.all_gather(jnp.concatenate([row, col], axis=0), 'src', axis=0, axis_i...  5.2 us
    all_gather x1, blocking collectives, local(): both = lax.all_gather(averages, 'src', axis=0, axis_index_groups=pairs)  1.78 us
  transfers between devices with their start and end apart: 2, of which 1 were waited for; matrix products, arithmetic and copies ran while one was open for 0% of the time, Pallas kernels for 1%

profile of v6, /device:TPU:1, one launch (start us, length us, event | category | flops | bytes accessed | tf_op | source)
XLA Modules:
  0.0 67.6 jit_solution(8006952113211726423)
XLA Ops:
  0.6 0.0 copy-start.2
  0.6 11.5 %collective-permute-start = (bf16[64,256]{1,0:T(8,128)(2,1)}, bf16[64,256]{1,0:T(8,128)(2,1)S(1)}, u32[]{:S(2)}, u32[]{:S(2)}) collective-permute-start(bf16[64,256]{1,0:T(8,128)(2,1)} %bitcast.30), channel_id=1, source_target_pairs={{0,8},{1,9},{2,10},{3,11},{4,12},{5,13},{6,14},{7,15},{8,0},{9,1},... | collective-permute-start | bytes 98312 | tf_op jit(solution)/shard_map/ppermute | solution.py:101
  12.1 0.0 copy-done.2
  12.1 0.0 copy-start.3
  12.1 10.2 %conditional.1 = (bf16[8,32,256]{2,1,0:T(8,128)(2,1)S(1)}) conditional(s32[]{:T(128)} %convert_element_type.3, bf16[32,256]{1,0:T(8,128)(2,1)S(1)} %bitcast.28, bf16[32,256]{1,0:T(8,128)(2,1)S(1)} %bitcast.29), branch_computations={%region_0.1_spmd, %region_1.2_spmd} | conditional | bytes 409608 | solution.py:103
  12.2 10.2 %all_to_all.14 = bf16[8,32,256]{2,1,0:T(8,128)(2,1)S(1)} all-to-all(bf16[8,32,256]{2,1,0:T(8,128)(2,1)S(1)} %broadcast_in_dim.8), channel_id=1, replica_groups={{0,32,64,96,128,160,192,224},{16,48,80,112,144,176,208,240},{256,288,32..., dimensions={0} | all-to-all | bytes 262144 | tf_op jit(solution)/shard_map/cond/branch_1_fun/all_to_all | solution.py:105
  22.3 0.0 collective-permute-done
  22.3 0.0 copy-done.3
  22.3 0.8 %broadcast_in_dim.12 = bf16[8,2,64,256]{3,2,1,0:T(8,128)(2,1)} broadcast(bf16[2,64,256]{2,1,0:T(8,128)(2,1)S(1)} %pad_maximum_fusion), dimensions={1,2,3} | broadcast | bytes 589824 | tf_op jit(solution)/shard_map/broadcast_in_dim | solution.py:17
  23.2 6.8 %all-to-all-start.1 = ((bf16[8,2,64,256]{3,2,1,0:T(8,128)(2,1)}), bf16[8,2,64,256]{3,2,1,0:T(8,128)(2,1)S(1)}, u32[]{:S(2)}, u32[]{:S(2)}) async-start(bf16[8,2,64,256]{3,2,1,0:T(8,128)(2,1)} %broadcast_in_dim.12), calls=%async_computation.1 | async-start | bytes 1048576 | tf_op jit(solution)/shard_map/all_to_all | solution.py:111
  30.0 0.1 pad_add_fusion.start_ref
  30.1 6.8 %all-gather.1 = bf16[16,32,256]{2,1,0:T(8,128)(2,1)S(1)} all-gather(bf16[8,32,256]{2,1,0:T(8,128)(2,1)S(1)} %get-tuple-element.36), channel_id=3, replica_groups={{0,256},{16,272},{32,288},{48,304},{64,320},{80,336},{96,352},{112,368}..., dimensions={0}, use_global_device_ids=true | all-gather | bytes 393216 | tf_op jit(solution)/shard_map/all_gather | solution.py:113
  36.9 0.0 copy-start
  36.9 0.0 copy-start.1
  36.9 5.7 %all-gather.2 = bf16[4,8,32,256]{3,2,1,0:T(8,128)(2,1)S(1)} all-gather(bf16[2,8,32,256]{3,2,1,0:T(8,128)(2,1)S(1)} %bitcast.26), channel_id=4, replica_groups={{0,16},{32,48},{64,80},{96,112},{128,144},{160,176},{192,208},{224,240}..., dimensions={0}, use_global_device_ids=true | all-gather | bytes 786432 | tf_op jit(solution)/shard_map/all_gather | solution.py:114
  42.6 0.0 copy-done
  42.6 0.0 copy-done.1
  42.6 0.8 %shard_map.67 = (bf16[1024,256]{1,0:T(8,128)(2,1)S(1)}, f32[1,256]{1,0:T(1,128)S(1)}, s32[256,128]{1,0:T(8,128)S(1)}, s32[256,128]{1,0:T(8,128)S(1)}) custom-call(s32[3]{0:T(128)S(1)} %pad_add_fusion.start_ref, bf16[2,2,8,32,256]{4,3,2,1,0:T(8,128)(2,1)S(1)} %bitcast.22, s32[16,256]{1,0:T(8,128)S(1)} %bitcast.24, s32[16,256]{1,0:T(8,128)S(1)} %bitcast.25), custom_call_target="tpu_custom_call" | custom-call | flops 1000000 | bytes 1048576 | tf_op jit(solution)/shard_map/pallas_call | solution.py:118
  43.4 1.3 %all-to-all-done.1 = bf16[8,2,64,256]{3,2,1,0:T(8,128)(2,1)S(1)} async-done(((bf16[8,2,64,256]{3,2,1,0:T(8,128)(2,1)}), bf16[8,2,64,256]{3,2,1,0:T(8,128)(2,1)S(1)}, u32[]{:S(2)}, u32[]{:S(2)}) %all-to-all-start.1) | async-done | bytes 524320 | tf_op jit(solution)/shard_map/all_to_all | solution.py:111
  44.7 1.1 %shard_map.68 = (f32[256,256]{1,0:T(8,128)S(1)}, f32[1,256]{1,0:T(1,128)S(1)}, f32[1,256]{1,0:T(1,128)S(1)}) custom-call(bf16[1024,256]{1,0:T(8,128)(2,1)S(1)} %bitcast.23, bf16[1024,256]{1,0:T(8,128)(2,1)S(1)} %get-tuple-element.24.t_ref, f32[1,256]{1,0:T(1,128)S(1)} %get-tuple-element.25.scale_ref, s32[256,128]{1,0:T(8,128)S(1)} %get-tuple-element.26.lanes_t_ref, ...), custom_call_target="tpu_custom_call" | custom-call | flops 300000000 | bytes 2097152 | tf_op jit(solution)/shard_map/pallas_call | solution.py:131
  45.8 5.2 %all-gather.5 = f32[2,2,256]{2,1,0:T(2,128)S(1)} all-gather(f32[1,2,256]{2,1,0:T(2,128)S(1)} %maximum_bitcast_fusion), channel_id=5, replica_groups={{0,16},{32,48},{64,80},{96,112},{128,144},{160,176},{192,208},{224,240}..., dimensions={0}, use_global_device_ids=true | all-gather | bytes 6144 | tf_op jit(solution)/shard_map/all_gather | solution.py:145
  51.1 13.8 %all_to_all.15 = f32[16,2,256]{2,1,0:T(2,128)S(1)} all-to-all(f32[16,2,256]{2,1,0:T(2,128)S(1)} %broadcast_in_dim.14), channel_id=1, replica_groups={{16,17,18,19,20,21,22,23,24,25,26,27,28,29,30,31},{48,49,50,51,52,53,54..., dimensions={0} | all-to-all | bytes 65536 | tf_op jit(solution)/shard_map/all_to_all | solution.py:149
  64.9 1.8 %all-gather.6.both_ref = f32[2,2,256]{2,1,0:T(2,128)S(1)} all-gather(f32[1,2,256]{2,1,0:T(2,128)S(1)} %multiply_bitcast_fusion), channel_id=6, replica_groups={{0,16},{32,48},{64,80},{96,112},{128,144},{160,176},{192,208},{224,240}..., dimensions={0}, use_global_device_ids=true | all-gather | bytes 6144 | tf_op jit(solution)/shard_map/all_gather | solution.py:151
  66.7 0.9 %shard_map.69 = (bf16[256,256]{1,0:T(8,128)(2,1)}, f32[1,256]{1,0:T(1,128)}, f32[1,256]{1,0:T(1,128)}) custom-call(s32[1]{0:T(128)} %bitcast.1.core_ref, f32[2,2,256]{2,1,0:T(2,128)S(1)} %all-gather.6.both_ref, f32[256,256]{1,0:T(8,128)S(1)} %get-tuple-element.30.cos_ref), custom_call_target="tpu_custom_call" | custom-call | flops 200000 | bytes 524288 | tf_op jit(solution)/shard_map/pallas_call | solution.py:152
  (8 shorter events, 0.1 us)
Async XLA Ops:
  0.6 11.5 %copy-start.2 = (bf16[256,32]{0,1:T(8,128)(2,1)S(1)}, bf16[256,32]{0,1:T(8,128)(2,1)}, u32[]{:S(2)}) copy-start(bf16[256,32]{0,1:T(8,128)(2,1)} %param.7) | copy-start | bytes 49156
  0.6 21.7 %collective-permute-start = (bf16[64,256]{1,0:T(8,128)(2,1)}, bf16[64,256]{1,0:T(8,128)(2,1)S(1)}, u32[]{:S(2)}, u32[]{:S(2)}) collective-permute-start(bf16[64,256]{1,0:T(8,128)(2,1)} %bitcast.30), channel_id=1, source_target_pairs={{0,8},{1,9},{2,10},{3,11},{4,12},{5,13},{6,14},{7,15},{8,0},{9,1},... | collective-permute-start | bytes 98312 | tf_op jit(solution)/shard_map/ppermute | solution.py:101
  12.1 10.2 %copy-start.3 = (bf16[256,64]{0,1:T(8,128)(2,1)S(1)}, bf16[256,64]{0,1:T(8,128)(2,1)}, u32[]{:S(2)}) copy-start(bf16[256,64]{0,1:T(8,128)(2,1)} %param.6) | copy-start | bytes 98308
  23.2 21.5 %all-to-all-start.1 = ((bf16[8,2,64,256]{3,2,1,0:T(8,128)(2,1)}), bf16[8,2,64,256]{3,2,1,0:T(8,128)(2,1)S(1)}, u32[]{:S(2)}, u32[]{:S(2)}) async-start(bf16[8,2,64,256]{3,2,1,0:T(8,128)(2,1)} %broadcast_in_dim.12), calls=%async_computation.1 | async-start | bytes 1048576 | tf_op jit(solution)/shard_map/all_to_all | solution.py:111
  36.9 5.7 %copy-start = (s32[256,16]{0,1:T(8,128)S(1)}, s32[256,16]{0,1:T(8,128)}, u32[]{:S(2)}) copy-start(s32[256,16]{0,1:T(8,128)} %param.8) | copy-start | bytes 49156
  36.9 5.7 %copy-start.1 = (s32[256,16]{0,1:T(8,128)S(1)}, s32[256,16]{0,1:T(8,128)}, u32[]{:S(2)}) copy-start(s32[256,16]{0,1:T(8,128)} %param.9) | copy-start | bytes 49156

commit v7 on v6

--- a/solution.py
+++ b/solution.py
@@ -1,3 +1,4 @@
+import functools
 import itertools
 
 import jax
@@ -22,33 +23,31 @@
     return lax.rsqrt(jnp.sum(wide * wide, axis=0, keepdims=True) + EPSILON)
 
 
-def picked(cosines, index):
+def picked(cosines, index, first, count):
     total = jnp.zeros(index.shape, jnp.float32)
     for half in range(cosines.shape[1] // LANES):
         block = cosines[:, half * LANES : (half + 1) * LANES]
         found = jnp.take_along_axis(block, index & (LANES - 1), axis=1)
-        total = total + jnp.where(index >> 7 == half, found, 0.0)
-    return jnp.sum(total.T, axis=0, keepdims=True)
+        total = jnp.where(index >> 7 == half, found, total)
+    return jnp.sum(total.T[first : first + count], axis=0, keepdims=True)
 
 
-def lanes_of(near, start):
-    count, rows = near.shape
-    fill = jnp.full((LANES - count, rows), -1, jnp.int32)
-    return jnp.concatenate([near - start, fill], axis=0).T
+def lanes_of(near_t, near_s):
+    fill = jnp.full((LANES - near_t.shape[0] - near_s.shape[0], near_t.shape[1]), -1, jnp.int32)
+    return jnp.concatenate([near_t, near_s, fill], axis=0).T
 
 
-def target_kernel(start_ref, t_ref, near_t_ref, near_s_ref, ordered_ref, scale_ref, lanes_t_ref, lanes_s_ref):
+def target_kernel(start_ref, t_ref, near_t_ref, near_s_ref, ordered_ref, scale_ref, lanes_ref):
     layer = start_ref[2]
     order = itertools.product(range(t_ref.shape[2]), range(2), range(t_ref.shape[0]))
     pieces = [t_ref[c, lax.rem(layer + h, 2), p] for p, h, c in order]
     targets = jnp.concatenate(pieces, axis=0)
     ordered_ref[...] = targets
     scale_ref[...] = inverse_norms(targets)
-    lanes_t_ref[...] = lanes_of(near_t_ref[...], start_ref[0])
-    lanes_s_ref[...] = lanes_of(near_s_ref[...], start_ref[1])
+    lanes_ref[...] = lanes_of(near_t_ref[...] - start_ref[0], near_s_ref[...] - start_ref[1])
 
 
-def tile_kernel(s_ref, t_ref, scale_ref, lanes_t_ref, lanes_s_ref, cos_ref, row_ref, col_ref):
+def tile_kernel(near_count, s_ref, t_ref, scale_ref, lanes_ref, cos_ref, row_ref, col_ref):
     sources = s_ref[...]
     targets = t_ref[...]
     s_scale = inverse_norms(sources)
@@ -57,8 +56,9 @@
     products = lax.dot_general(sources, targets, MAJOR, preferred_element_type=jnp.float32)
     cosines = products * column * scale_ref[...]
     cos_ref[...] = cosines
-    row_ref[...] = picked(cosines, lanes_t_ref[...])
-    col_ref[...] = picked(cosines.T, lanes_s_ref[...])
+    lanes = lanes_ref[...]
+    row_ref[...] = picked(cosines, lanes, 0, near_count)
+    col_ref[...] = picked(cosines.T, lanes, near_count, near_count)
 
 
 def margin_kernel(core_ref, both_ref, cos_ref, margin_ref, src_ref, tgt_ref):
@@ -115,22 +115,21 @@
     smem = pl.BlockSpec(memory_space=pltpu.SMEM)
     vmem = pl.BlockSpec(memory_space=pltpu.VMEM)
     wide = (src_count, LANES)
-    targets, scale, lanes_t, lanes_s = pl.pallas_call(
+    targets, scale, lanes = pl.pallas_call(
         target_kernel,
         in_specs=[smem] + [vmem] * 3,
-        out_specs=[vmem] * 4,
+        out_specs=[vmem] * 3,
         out_shape=[
             jax.ShapeDtypeStruct((source.shape[0], tgt_count), jnp.bfloat16),
             jax.ShapeDtypeStruct((1, tgt_count), jnp.float32),
             jax.ShapeDtypeStruct(wide, jnp.int32),
-            jax.ShapeDtypeStruct((tgt_count, LANES), jnp.int32),
         ],
         compiler_params=pltpu.CompilerParams(vmem_limit_bytes=32 * 1024 * 1024),
         cost_estimate=pl.CostEstimate(flops=1_000_000, bytes_accessed=2**20, transcendentals=256),
     )(starts, halves, src_near.T, tgt_near.T)
     cosines, row, col = pl.pallas_call(
-        tile_kernel,
-        in_specs=[vmem] * 5,
+        functools.partial(tile_kernel, near_count),
+        in_specs=[vmem] * 4,
         out_specs=[vmem] * 3,
         out_shape=[
             jax.ShapeDtypeStruct((src_count, tgt_count), jnp.float32),
@@ -139,7 +138,7 @@
         ],
         compiler_params=pltpu.CompilerParams(vmem_limit_bytes=32 * 1024 * 1024),
         cost_estimate=pl.CostEstimate(flops=300_000_000, bytes_accessed=2**21, transcendentals=512),
-    )(source, targets, scale, lanes_t, lanes_s)
+    )(source, targets, scale, lanes)
 
     by_rows = core == 1
     both = lax.all_gather(

time: 68.1 us -> 68.1 us (level)
  no operation moved by 1% of the time
where the time goes in v7:
time: 68.1 us; the launch traced here: 67.6 us
  blocking collectives  43.5 us (64%)
  starting transfers between devices  18.3 us (27%)
  Pallas kernels  2.73 us (4%)
  waiting for transfers between devices  1.33 us (2%)
  local copies, waits for them, and re-layouts  0.88 us (1%)
  between operations  0.7 us (1%)
    all_to_all x1, blocking collectives, local(): lax.all_to_all(spread(sums, chips), ('src', 'tgt'), 0, 0, axis_index_grou...  13.8 us
    ppermute x1, starting transfers between devices, local(): partner = lax.ppermute(mine, 'tgt', partners)  11.5 us
    all_to_all x1, blocking collectives, local(): lax.all_to_all(spread(part, copies), 'src', 0, 0, axis_index_groups=blocks)  10.2 us
    all_to_all x1, starting transfers between devices, local(): source = lax.all_to_all(operand, 'tgt', 0, 0, axis_index_groups=lines_y)  6.82 us
    all_gather x1, blocking collectives, local(): halves = lax.all_gather(own, 'src', axis=0, axis_index_groups=far_pairs)  6.79 us
    all_gather x1, blocking collectives, local(): halves = lax.all_gather(halves, 'src', axis=0, axis_index_groups=pairs)  5.74 us
    all_gather x1, blocking collectives, local(): lax.all_gather(jnp.concatenate([row, col], axis=0), 'src', axis=0, axis_i...  5.2 us
    all_gather x1, blocking collectives, local(): both = lax.all_gather(averages, 'src', axis=0, axis_index_groups=pairs)  1.78 us
  transfers between devices with their start and end apart: 2, of which 1 were waited for; matrix products, arithmetic and copies ran while one was open for 0% of the time, Pallas kernels for 1%

profile of v7, /device:TPU:1, one launch (start us, length us, event | category | flops | bytes accessed | tf_op | source)
XLA Modules:
  0.0 67.6 jit_solution(15051586496930267201)
XLA Ops:
  0.6 0.0 copy-start.2
  0.6 11.5 %collective-permute-start = (bf16[64,256]{1,0:T(8,128)(2,1)}, bf16[64,256]{1,0:T(8,128)(2,1)S(1)}, u32[]{:S(2)}, u32[]{:S(2)}) collective-permute-start(bf16[64,256]{1,0:T(8,128)(2,1)} %bitcast.30), channel_id=1, source_target_pairs={{0,8},{1,9},{2,10},{3,11},{4,12},{5,13},{6,14},{7,15},{8,0},{9,1},... | collective-permute-start | bytes 98312 | tf_op jit(solution)/shard_map/ppermute | solution.py:101
  12.1 0.0 copy-done.2
  12.1 0.0 copy-start.3
  12.1 10.2 %conditional.1 = (bf16[8,32,256]{2,1,0:T(8,128)(2,1)S(1)}) conditional(s32[]{:T(128)} %convert_element_type.3, bf16[32,256]{1,0:T(8,128)(2,1)S(1)} %bitcast.28, bf16[32,256]{1,0:T(8,128)(2,1)S(1)} %bitcast.29), branch_computations={%region_0.1_spmd, %region_1.2_spmd} | conditional | bytes 409608 | solution.py:103
  12.2 10.2 %all_to_all.14 = bf16[8,32,256]{2,1,0:T(8,128)(2,1)S(1)} all-to-all(bf16[8,32,256]{2,1,0:T(8,128)(2,1)S(1)} %broadcast_in_dim.8), channel_id=1, replica_groups={{0,32,64,96,128,160,192,224},{16,48,80,112,144,176,208,240},{256,288,32..., dimensions={0} | all-to-all | bytes 262144 | tf_op jit(solution)/shard_map/cond/branch_1_fun/all_to_all | solution.py:105
  22.3 0.0 collective-permute-done
  22.3 0.0 copy-done.3
  22.3 0.8 %broadcast_in_dim.12 = bf16[8,2,64,256]{3,2,1,0:T(8,128)(2,1)} broadcast(bf16[2,64,256]{2,1,0:T(8,128)(2,1)S(1)} %pad_maximum_fusion), dimensions={1,2,3} | broadcast | bytes 589824 | tf_op jit(solution)/shard_map/broadcast_in_dim | solution.py:18
  23.2 6.8 %all-to-all-start.1 = ((bf16[8,2,64,256]{3,2,1,0:T(8,128)(2,1)}), bf16[8,2,64,256]{3,2,1,0:T(8,128)(2,1)S(1)}, u32[]{:S(2)}, u32[]{:S(2)}) async-start(bf16[8,2,64,256]{3,2,1,0:T(8,128)(2,1)} %broadcast_in_dim.12), calls=%async_computation.1 | async-start | bytes 1048576 | tf_op jit(solution)/shard_map/all_to_all | solution.py:111
  30.0 0.1 pad_add_fusion.start_ref
  30.1 6.8 %all-gather.1 = bf16[16,32,256]{2,1,0:T(8,128)(2,1)S(1)} all-gather(bf16[8,32,256]{2,1,0:T(8,128)(2,1)S(1)} %get-tuple-element.34), channel_id=3, replica_groups={{0,256},{16,272},{32,288},{48,304},{64,320},{80,336},{96,352},{112,368}..., dimensions={0}, use_global_device_ids=true | all-gather | bytes 393216 | tf_op jit(solution)/shard_map/all_gather | solution.py:113
  36.9 0.0 copy-start
  36.9 0.0 copy-start.1
  36.9 5.7 %all-gather.2 = bf16[4,8,32,256]{3,2,1,0:T(8,128)(2,1)S(1)} all-gather(bf16[2,8,32,256]{3,2,1,0:T(8,128)(2,1)S(1)} %bitcast.26), channel_id=4, replica_groups={{0,16},{32,48},{64,80},{96,112},{128,144},{160,176},{192,208},{224,240}..., dimensions={0}, use_global_device_ids=true | all-gather | bytes 786432 | tf_op jit(solution)/shard_map/all_gather | solution.py:114
  42.6 0.0 copy-done
  42.6 0.0 copy-done.1
  42.6 0.8 %shard_map.67 = (bf16[1024,256]{1,0:T(8,128)(2,1)S(1)}, f32[1,256]{1,0:T(1,128)S(1)}, s32[256,128]{1,0:T(8,128)S(1)}) custom-call(s32[3]{0:T(128)S(1)} %pad_add_fusion.start_ref, bf16[2,2,8,32,256]{4,3,2,1,0:T(8,128)(2,1)S(1)} %bitcast.22, s32[16,256]{1,0:T(8,128)S(1)} %bitcast.24, s32[16,256]{1,0:T(8,128)S(1)} %bitcast.25), custom_call_target="tpu_custom_call" | custom-call | flops 1000000 | bytes 1048576 | tf_op jit(solution)/shard_map/pallas_call | solution.py:118
  43.4 1.3 %all-to-all-done.1 = bf16[8,2,64,256]{3,2,1,0:T(8,128)(2,1)S(1)} async-done(((bf16[8,2,64,256]{3,2,1,0:T(8,128)(2,1)}), bf16[8,2,64,256]{3,2,1,0:T(8,128)(2,1)S(1)}, u32[]{:S(2)}, u32[]{:S(2)}) %all-to-all-start.1) | async-done | bytes 524320 | tf_op jit(solution)/shard_map/all_to_all | solution.py:111
  44.7 1.0 %shard_map.68 = (f32[256,256]{1,0:T(8,128)S(1)}, f32[1,256]{1,0:T(1,128)S(1)}, f32[1,256]{1,0:T(1,128)S(1)}) custom-call(bf16[1024,256]{1,0:T(8,128)(2,1)S(1)} %bitcast.23, bf16[1024,256]{1,0:T(8,128)(2,1)S(1)} %get-tuple-element.23.t_ref, f32[1,256]{1,0:T(1,128)S(1)} %get-tuple-element.24.scale_ref, s32[256,128]{1,0:T(8,128)S(1)} %get-tuple-element.25.lanes_ref), custom_call_target="tpu_custom_call" | custom-call | flops 300000000 | bytes 2097152 | tf_op jit(solution)/shard_map/pallas_call | solution.py:130
  45.8 5.2 %all-gather.5 = f32[2,2,256]{2,1,0:T(2,128)S(1)} all-gather(f32[1,2,256]{2,1,0:T(2,128)S(1)} %maximum_bitcast_fusion), channel_id=5, replica_groups={{0,16},{32,48},{64,80},{96,112},{128,144},{160,176},{192,208},{224,240}..., dimensions={0}, use_global_device_ids=true | all-gather | bytes 6144 | tf_op jit(solution)/shard_map/all_gather | solution.py:144
  51.0 13.8 %all_to_all.15 = f32[16,2,256]{2,1,0:T(2,128)S(1)} all-to-all(f32[16,2,256]{2,1,0:T(2,128)S(1)} %broadcast_in_dim.14), channel_id=1, replica_groups={{16,17,18,19,20,21,22,23,24,25,26,27,28,29,30,31},{48,49,50,51,52,53,54..., dimensions={0} | all-to-all | bytes 65536 | tf_op jit(solution)/shard_map/all_to_all | solution.py:148
  64.9 1.8 %all-gather.6.both_ref = f32[2,2,256]{2,1,0:T(2,128)S(1)} all-gather(f32[1,2,256]{2,1,0:T(2,128)S(1)} %multiply_bitcast_fusion), channel_id=6, replica_groups={{0,16},{32,48},{64,80},{96,112},{128,144},{160,176},{192,208},{224,240}..., dimensions={0}, use_global_device_ids=true | all-gather | bytes 6144 | tf_op jit(solution)/shard_map/all_gather | solution.py:150
  66.7 0.9 %shard_map.69 = (bf16[256,256]{1,0:T(8,128)(2,1)}, f32[1,256]{1,0:T(1,128)}, f32[1,256]{1,0:T(1,128)}) custom-call(s32[1]{0:T(128)} %bitcast.1.core_ref, f32[2,2,256]{2,1,0:T(2,128)S(1)} %all-gather.6.both_ref, f32[256,256]{1,0:T(8,128)S(1)} %get-tuple-element.28.cos_ref), custom_call_target="tpu_custom_call" | custom-call | flops 200000 | bytes 524288 | tf_op jit(solution)/shard_map/pallas_call | solution.py:151
  (8 shorter events, 0.1 us)
Async XLA Ops:
  0.6 11.5 %copy-start.2 = (bf16[256,32]{0,1:T(8,128)(2,1)S(1)}, bf16[256,32]{0,1:T(8,128)(2,1)}, u32[]{:S(2)}) copy-start(bf16[256,32]{0,1:T(8,128)(2,1)} %param.7) | copy-start | bytes 49156
  0.6 21.7 %collective-permute-start = (bf16[64,256]{1,0:T(8,128)(2,1)}, bf16[64,256]{1,0:T(8,128)(2,1)S(1)}, u32[]{:S(2)}, u32[]{:S(2)}) collective-permute-start(bf16[64,256]{1,0:T(8,128)(2,1)} %bitcast.30), channel_id=1, source_target_pairs={{0,8},{1,9},{2,10},{3,11},{4,12},{5,13},{6,14},{7,15},{8,0},{9,1},... | collective-permute-start | bytes 98312 | tf_op jit(solution)/shard_map/ppermute | solution.py:101
  12.1 10.2 %copy-start.3 = (bf16[256,64]{0,1:T(8,128)(2,1)S(1)}, bf16[256,64]{0,1:T(8,128)(2,1)}, u32[]{:S(2)}) copy-start(bf16[256,64]{0,1:T(8,128)(2,1)} %param.6) | copy-start | bytes 98308
  23.2 21.5 %all-to-all-start.1 = ((bf16[8,2,64,256]{3,2,1,0:T(8,128)(2,1)}), bf16[8,2,64,256]{3,2,1,0:T(8,128)(2,1)S(1)}, u32[]{:S(2)}, u32[]{:S(2)}) async-start(bf16[8,2,64,256]{3,2,1,0:T(8,128)(2,1)} %broadcast_in_dim.12), calls=%async_computation.1 | async-start | bytes 1048576 | tf_op jit(solution)/shard_map/all_to_all | solution.py:111
  36.9 5.7 %copy-start = (s32[256,16]{0,1:T(8,128)S(1)}, s32[256,16]{0,1:T(8,128)}, u32[]{:S(2)}) copy-start(s32[256,16]{0,1:T(8,128)} %param.8) | copy-start | bytes 49156
  36.9 5.7 %copy-start.1 = (s32[256,16]{0,1:T(8,128)S(1)}, s32[256,16]{0,1:T(8,128)}, u32[]{:S(2)}) copy-start(s32[256,16]{0,1:T(8,128)} %param.9) | copy-start | bytes 49156

commit v8 on v7

--- a/solution.py
+++ b/solution.py
@@ -47,7 +47,7 @@
     lanes_ref[...] = lanes_of(near_t_ref[...] - start_ref[0], near_s_ref[...] - start_ref[1])
 
 
-def tile_kernel(near_count, s_ref, t_ref, scale_ref, lanes_ref, cos_ref, row_ref, col_ref):
+def tile_kernel(near_count, s_ref, t_ref, scale_ref, lanes_ref, cos_ref, sums_ref):
     sources = s_ref[...]
     targets = t_ref[...]
     s_scale = inverse_norms(sources)
@@ -57,18 +57,27 @@
     cosines = products * column * scale_ref[...]
     cos_ref[...] = cosines
     lanes = lanes_ref[...]
-    row_ref[...] = picked(cosines, lanes, 0, near_count)
-    col_ref[...] = picked(cosines.T, lanes, near_count, near_count)
+    by_row = picked(cosines, lanes, 0, near_count)
+    by_column = picked(cosines.T, lanes, near_count, near_count)
+    sums_ref[...] = jnp.concatenate([by_row, by_column], axis=0)
 
 
-def margin_kernel(core_ref, both_ref, cos_ref, margin_ref, src_ref, tgt_ref):
+def margin_kernel(core_ref, both_ref, cos_ref, margin_ref, src_ref, tgt_ref, staged, sems):
     src_average = both_ref[1, pl.ds(core_ref[0], 1)]
     tgt_average = both_ref[0, :1]
     src_ref[...] = src_average
     tgt_ref[...] = tgt_average
     rows = src_average.shape[1]
     column = jnp.broadcast_to(src_average, (8, rows)).T[:, :1]
-    margin_ref[...] = (cos_ref[...] / ((column + tgt_average) / 2.0)).astype(jnp.bfloat16)
+    half = rows // 2
+    copies = []
+    for k in range(2):
+        part = slice(k * half, (k + 1) * half)
+        staged[part] = (cos_ref[part] / ((column[part] + tgt_average) / 2.0)).astype(jnp.bfloat16)
+        copies.append(pltpu.make_async_copy(staged.at[part], margin_ref.at[part], sems.at[k]))
+        copies[k].start()
+    for copy in copies:
+        copy.wait()
 
 
 def local(src_embed, tgt_embed, src_near, tgt_near):
@@ -127,23 +136,20 @@
         compiler_params=pltpu.CompilerParams(vmem_limit_bytes=32 * 1024 * 1024),
         cost_estimate=pl.CostEstimate(flops=1_000_000, bytes_accessed=2**20, transcendentals=256),
     )(starts, halves, src_near.T, tgt_near.T)
-    cosines, row, col = pl.pallas_call(
+    cosines, sums = pl.pallas_call(
         functools.partial(tile_kernel, near_count),
         in_specs=[vmem] * 4,
-        out_specs=[vmem] * 3,
+        out_specs=[vmem] * 2,
         out_shape=[
             jax.ShapeDtypeStruct((src_count, tgt_count), jnp.float32),
-            jax.ShapeDtypeStruct((1, src_count), jnp.float32),
-            jax.ShapeDtypeStruct((1, tgt_count), jnp.float32),
+            jax.ShapeDtypeStruct((2, src_count), jnp.float32),
         ],
         compiler_params=pltpu.CompilerParams(vmem_limit_bytes=32 * 1024 * 1024),
         cost_estimate=pl.CostEstimate(flops=300_000_000, bytes_accessed=2**21, transcendentals=512),
     )(source, targets, scale, lanes)
 
     by_rows = core == 1
-    both = lax.all_gather(
-        jnp.concatenate([row, col], axis=0), "src", axis=0, axis_index_groups=pairs
-    )
+    both = lax.all_gather(sums, "src", axis=0, axis_index_groups=pairs)
     sums = jnp.where(by_rows, both[:, 0], jnp.broadcast_to(jnp.sum(both[:, 1], axis=0), (2, tgt_count)))
     parts = lax.all_to_all(spread(sums, chips), ("src", "tgt"), 0, 0, axis_index_groups=lines)
     averages = jnp.sum(parts, axis=0) / near_count
@@ -151,11 +157,15 @@
     margin, src_average, tgt_average = pl.pallas_call(
         margin_kernel,
         in_specs=[smem] + [vmem] * 2,
-        out_specs=[vmem] * 3,
+        out_specs=[pl.BlockSpec(memory_space=pl.ANY)] + [vmem] * 2,
         out_shape=[
             jax.ShapeDtypeStruct((src_count, tgt_count), jnp.bfloat16),
             jax.ShapeDtypeStruct((1, src_count), jnp.float32),
             jax.ShapeDtypeStruct((1, tgt_count), jnp.float32),
+        ],
+        scratch_shapes=[
+            pltpu.VMEM((src_count, tgt_count), jnp.bfloat16),
+            pltpu.SemaphoreType.DMA((2,)),
         ],
         compiler_params=pltpu.CompilerParams(vmem_limit_bytes=8 * 1024 * 1024),
         cost_estimate=pl.CostEstimate(flops=200_000, bytes_accessed=2**19, transcendentals=0),

time: 68.1 us -> 68.6 us (level)
  no operation moved by 1% of the time
where the time goes in v8:
time: 68.6 us; the launch traced here: 68.2 us
  blocking collectives  43.5 us (63%)
  starting transfers between devices  18.3 us (27%)
  Pallas kernels  3.31 us (5%)
  waiting for transfers between devices  1.33 us (2%)
  local copies, waits for them, and re-layouts  0.88 us (1%)
  between operations  0.69 us (1%)
    all_to_all x1, blocking collectives, local(): lax.all_to_all(spread(sums, chips), ('src', 'tgt'), 0, 0, axis_index_grou...  13.8 us
    ppermute x1, starting transfers between devices, local(): partner = lax.ppermute(mine, 'tgt', partners)  11.5 us
    all_to_all x1, blocking collectives, local(): lax.all_to_all(spread(part, copies), 'src', 0, 0, axis_index_groups=blocks)  10.2 us
    all_to_all x1, starting transfers between devices, local(): source = lax.all_to_all(operand, 'tgt', 0, 0, axis_index_groups=lines_y)  6.82 us
    all_gather x1, blocking collectives, local(): halves = lax.all_gather(own, 'src', axis=0, axis_index_groups=far_pairs)  6.79 us
    all_gather x1, blocking collectives, local(): halves = lax.all_gather(halves, 'src', axis=0, axis_index_groups=pairs)  5.74 us
    all_gather x1, blocking collectives, local(): both = lax.all_gather(sums, 'src', axis=0, axis_index_groups=pairs)  5.2 us
    all_gather x1, blocking collectives, local(): both = lax.all_gather(averages, 'src', axis=0, axis_index_groups=pairs)  1.78 us
  transfers between devices with their start and end apart: 2, of which 1 were waited for; matrix products, arithmetic and copies ran while one was open for 0% of the time, Pallas kernels for 1%

profile of v8, /device:TPU:1, one launch (start us, length us, event | category | flops | bytes accessed | tf_op | source)
XLA Modules:
  0.0 68.2 jit_solution(3657455042332390484)
XLA Ops:
  0.6 0.0 copy-start.2
  0.6 11.5 %collective-permute-start = (bf16[64,256]{1,0:T(8,128)(2,1)}, bf16[64,256]{1,0:T(8,128)(2,1)S(1)}, u32[]{:S(2)}, u32[]{:S(2)}) collective-permute-start(bf16[64,256]{1,0:T(8,128)(2,1)} %bitcast.30), channel_id=1, source_target_pairs={{0,8},{1,9},{2,10},{3,11},{4,12},{5,13},{6,14},{7,15},{8,0},{9,1},... | collective-permute-start | bytes 98312 | tf_op jit(solution)/shard_map/ppermute | solution.py:110
  12.1 0.0 copy-done.2
  12.1 0.0 copy-start.3
  12.1 10.2 %conditional.1 = (bf16[8,32,256]{2,1,0:T(8,128)(2,1)S(1)}) conditional(s32[]{:T(128)} %convert_element_type.3, bf16[32,256]{1,0:T(8,128)(2,1)S(1)} %bitcast.28, bf16[32,256]{1,0:T(8,128)(2,1)S(1)} %bitcast.29), branch_computations={%region_0.1_spmd, %region_1.2_spmd} | conditional | bytes 409608 | solution.py:112
  12.2 10.2 %all_to_all.14 = bf16[8,32,256]{2,1,0:T(8,128)(2,1)S(1)} all-to-all(bf16[8,32,256]{2,1,0:T(8,128)(2,1)S(1)} %broadcast_in_dim.8), channel_id=1, replica_groups={{0,32,64,96,128,160,192,224},{16,48,80,112,144,176,208,240},{256,288,32..., dimensions={0} | all-to-all | bytes 262144 | tf_op jit(solution)/shard_map/cond/branch_1_fun/all_to_all | solution.py:114
  22.3 0.0 collective-permute-done
  22.3 0.0 copy-done.3
  22.3 0.8 %broadcast_in_dim.12 = bf16[8,2,64,256]{3,2,1,0:T(8,128)(2,1)} broadcast(bf16[2,64,256]{2,1,0:T(8,128)(2,1)S(1)} %pad_maximum_fusion), dimensions={1,2,3} | broadcast | bytes 589824 | tf_op jit(solution)/shard_map/broadcast_in_dim | solution.py:18
  23.2 6.8 %all-to-all-start.1 = ((bf16[8,2,64,256]{3,2,1,0:T(8,128)(2,1)}), bf16[8,2,64,256]{3,2,1,0:T(8,128)(2,1)S(1)}, u32[]{:S(2)}, u32[]{:S(2)}) async-start(bf16[8,2,64,256]{3,2,1,0:T(8,128)(2,1)} %broadcast_in_dim.12), calls=%async_computation.1 | async-start | bytes 1048576 | tf_op jit(solution)/shard_map/all_to_all | solution.py:120
  30.0 0.1 pad_add_fusion.start_ref
  30.1 6.8 %all-gather.1 = bf16[16,32,256]{2,1,0:T(8,128)(2,1)S(1)} all-gather(bf16[8,32,256]{2,1,0:T(8,128)(2,1)S(1)} %get-tuple-element.32), channel_id=3, replica_groups={{0,256},{16,272},{32,288},{48,304},{64,320},{80,336},{96,352},{112,368}..., dimensions={0}, use_global_device_ids=true | all-gather | bytes 393216 | tf_op jit(solution)/shard_map/all_gather | solution.py:122
  36.9 0.0 copy-start
  36.9 0.0 copy-start.1
  36.9 5.7 %all-gather.2 = bf16[4,8,32,256]{3,2,1,0:T(8,128)(2,1)S(1)} all-gather(bf16[2,8,32,256]{3,2,1,0:T(8,128)(2,1)S(1)} %bitcast.26), channel_id=4, replica_groups={{0,16},{32,48},{64,80},{96,112},{128,144},{160,176},{192,208},{224,240}..., dimensions={0}, use_global_device_ids=true | all-gather | bytes 786432 | tf_op jit(solution)/shard_map/all_gather | solution.py:123
  42.6 0.0 copy-done
  42.6 0.0 copy-done.1
  42.6 0.8 %shard_map.67 = (bf16[1024,256]{1,0:T(8,128)(2,1)S(1)}, f32[1,256]{1,0:T(1,128)S(1)}, s32[256,128]{1,0:T(8,128)S(1)}) custom-call(s32[3]{0:T(128)S(1)} %pad_add_fusion.start_ref, bf16[2,2,8,32,256]{4,3,2,1,0:T(8,128)(2,1)S(1)} %bitcast.21, s32[16,256]{1,0:T(8,128)S(1)} %bitcast.23, s32[16,256]{1,0:T(8,128)S(1)} %bitcast.24), custom_call_target="tpu_custom_call" | custom-call | flops 1000000 | bytes 1048576 | tf_op jit(solution)/shard_map/pallas_call | solution.py:127
  43.4 1.3 %all-to-all-done.1 = bf16[8,2,64,256]{3,2,1,0:T(8,128)(2,1)S(1)} async-done(((bf16[8,2,64,256]{3,2,1,0:T(8,128)(2,1)}), bf16[8,2,64,256]{3,2,1,0:T(8,128)(2,1)S(1)}, u32[]{:S(2)}, u32[]{:S(2)}) %all-to-all-start.1) | async-done | bytes 524320 | tf_op jit(solution)/shard_map/all_to_all | solution.py:120
  44.7 1.0 %shard_map.68 = (f32[256,256]{1,0:T(8,128)S(1)}, f32[2,256]{1,0:T(2,128)S(1)}) custom-call(bf16[1024,256]{1,0:T(8,128)(2,1)S(1)} %bitcast.22, bf16[1024,256]{1,0:T(8,128)(2,1)S(1)} %get-tuple-element.22.t_ref, f32[1,256]{1,0:T(1,128)S(1)} %get-tuple-element.23.scale_ref, s32[256,128]{1,0:T(8,128)S(1)} %get-tuple-element.24.lanes_ref), custom_call_target="tpu_custom_call" | custom-call | flops 300000000 | bytes 2097152 | tf_op jit(solution)/shard_map/pallas_call | solution.py:139
  45.8 5.2 %all-gather.5 = f32[2,2,256]{2,1,0:T(2,128)S(1)} all-gather(f32[1,2,256]{2,1,0:T(2,128)S(1)} %bitcast.25), channel_id=5, replica_groups={{0,16},{32,48},{64,80},{96,112},{128,144},{160,176},{192,208},{224,240}..., dimensions={0}, use_global_device_ids=true | all-gather | bytes 6144 | tf_op jit(solution)/shard_map/all_gather | solution.py:152
  51.0 13.8 %all_to_all.15 = f32[16,2,256]{2,1,0:T(2,128)S(1)} all-to-all(f32[16,2,256]{2,1,0:T(2,128)S(1)} %broadcast_in_dim.14), channel_id=1, replica_groups={{16,17,18,19,20,21,22,23,24,25,26,27,28,29,30,31},{48,49,50,51,52,53,54..., dimensions={0} | all-to-all | bytes 65536 | tf_op jit(solution)/shard_map/all_to_all | solution.py:154
  64.9 1.8 %all-gather.6.both_ref = f32[2,2,256]{2,1,0:T(2,128)S(1)} all-gather(f32[1,2,256]{2,1,0:T(2,128)S(1)} %multiply_bitcast_fusion), channel_id=6, replica_groups={{0,16},{32,48},{64,80},{96,112},{128,144},{160,176},{192,208},{224,240}..., dimensions={0}, use_global_device_ids=true | all-gather | bytes 6144 | tf_op jit(solution)/shard_map/all_gather | solution.py:156
  66.7 1.5 %shard_map.69 = (bf16[256,256]{1,0:T(8,128)(2,1)}, f32[1,256]{1,0:T(1,128)}, f32[1,256]{1,0:T(1,128)}) custom-call(s32[1]{0:T(128)} %bitcast.1.core_ref, f32[2,2,256]{2,1,0:T(2,128)S(1)} %all-gather.6.both_ref, f32[256,256]{1,0:T(8,128)S(1)} %get-tuple-element.26.cos_ref), custom_call_target="tpu_custom_call" | custom-call | flops 200000 | bytes 524288 | tf_op jit(solution)/shard_map/pallas_call | solution.py:157
  (7 shorter events, 0.1 us)
Async XLA Ops:
  0.6 11.5 %copy-start.2 = (bf16[256,32]{0,1:T(8,128)(2,1)S(1)}, bf16[256,32]{0,1:T(8,128)(2,1)}, u32[]{:S(2)}) copy-start(bf16[256,32]{0,1:T(8,128)(2,1)} %param.7) | copy-start | bytes 49156
  0.6 21.7 %collective-permute-start = (bf16[64,256]{1,0:T(8,128)(2,1)}, bf16[64,256]{1,0:T(8,128)(2,1)S(1)}, u32[]{:S(2)}, u32[]{:S(2)}) collective-permute-start(bf16[64,256]{1,0:T(8,128)(2,1)} %bitcast.30), channel_id=1, source_target_pairs={{0,8},{1,9},{2,10},{3,11},{4,12},{5,13},{6,14},{7,15},{8,0},{9,1},... | collective-permute-start | bytes 98312 | tf_op jit(solution)/shard_map/ppermute | solution.py:110
  12.1 10.2 %copy-start.3 = (bf16[256,64]{0,1:T(8,128)(2,1)S(1)}, bf16[256,64]{0,1:T(8,128)(2,1)}, u32[]{:S(2)}) copy-start(bf16[256,64]{0,1:T(8,128)(2,1)} %param.6) | copy-start | bytes 98308
  23.2 21.5 %all-to-all-start.1 = ((bf16[8,2,64,256]{3,2,1,0:T(8,128)(2,1)}), bf16[8,2,64,256]{3,2,1,0:T(8,128)(2,1)S(1)}, u32[]{:S(2)}, u32[]{:S(2)}) async-start(bf16[8,2,64,256]{3,2,1,0:T(8,128)(2,1)} %broadcast_in_dim.12), calls=%async_computation.1 | async-start | bytes 1048576 | tf_op jit(solution)/shard_map/all_to_all | solution.py:120
  36.9 5.7 %copy-start = (s32[256,16]{0,1:T(8,128)S(1)}, s32[256,16]{0,1:T(8,128)}, u32[]{:S(2)}) copy-start(s32[256,16]{0,1:T(8,128)} %param.8) | copy-start | bytes 49156
  36.9 5.7 %copy-start.1 = (s32[256,16]{0,1:T(8,128)S(1)}, s32[256,16]{0,1:T(8,128)}, u32[]{:S(2)}) copy-start(s32[256,16]{0,1:T(8,128)} %param.9) | copy-start | bytes 49156

commit v9 on v8

--- a/solution.py
+++ b/solution.py
@@ -62,22 +62,14 @@
     sums_ref[...] = jnp.concatenate([by_row, by_column], axis=0)
 
 
-def margin_kernel(core_ref, both_ref, cos_ref, margin_ref, src_ref, tgt_ref, staged, sems):
+def margin_kernel(core_ref, both_ref, cos_ref, margin_ref, src_ref, tgt_ref):
     src_average = both_ref[1, pl.ds(core_ref[0], 1)]
     tgt_average = both_ref[0, :1]
     src_ref[...] = src_average
     tgt_ref[...] = tgt_average
     rows = src_average.shape[1]
     column = jnp.broadcast_to(src_average, (8, rows)).T[:, :1]
-    half = rows // 2
-    copies = []
-    for k in range(2):
-        part = slice(k * half, (k + 1) * half)
-        staged[part] = (cos_ref[part] / ((column[part] + tgt_average) / 2.0)).astype(jnp.bfloat16)
-        copies.append(pltpu.make_async_copy(staged.at[part], margin_ref.at[part], sems.at[k]))
-        copies[k].start()
-    for copy in copies:
-        copy.wait()
+    margin_ref[...] = (cos_ref[...] / ((column + tgt_average) / 2.0)).astype(jnp.bfloat16)
 
 
 def local(src_embed, tgt_embed, src_near, tgt_near):
@@ -157,15 +149,11 @@
     margin, src_average, tgt_average = pl.pallas_call(
         margin_kernel,
         in_specs=[smem] + [vmem] * 2,
-        out_specs=[pl.BlockSpec(memory_space=pl.ANY)] + [vmem] * 2,
+        out_specs=[vmem] * 3,
         out_shape=[
             jax.ShapeDtypeStruct((src_count, tgt_count), jnp.bfloat16),
             jax.ShapeDtypeStruct((1, src_count), jnp.float32),
             jax.ShapeDtypeStruct((1, tgt_count), jnp.float32),
-        ],
-        scratch_shapes=[
-            pltpu.VMEM((src_count, tgt_count), jnp.bfloat16),
-            pltpu.SemaphoreType.DMA((2,)),
         ],
         compiler_params=pltpu.CompilerParams(vmem_limit_bytes=8 * 1024 * 1024),
         cost_estimate=pl.CostEstimate(flops=200_000, bytes_accessed=2**19, transcendentals=0),

time: 68.6 us -> 68 us (level)
  no operation moved by 1% of the time
where the time goes in v9:
time: 68 us; the launch traced here: 67.6 us
  blocking collectives  43.5 us (64%)
  starting transfers between devices  18.3 us (27%)
  Pallas kernels  2.73 us (4%)
  waiting for transfers between devices  1.33 us (2%)
  local copies, waits for them, and re-layouts  0.88 us (1%)
  between operations  0.69 us (1%)
    all_to_all x1, blocking collectives, local(): lax.all_to_all(spread(sums, chips), ('src', 'tgt'), 0, 0, axis_index_grou...  13.8 us
    ppermute x1, starting transfers between devices, local(): partner = lax.ppermute(mine, 'tgt', partners)  11.5 us
    all_to_all x1, blocking collectives, local(): lax.all_to_all(spread(part, copies), 'src', 0, 0, axis_index_groups=blocks)  10.2 us
    all_to_all x1, starting transfers between devices, local(): source = lax.all_to_all(operand, 'tgt', 0, 0, axis_index_groups=lines_y)  6.82 us
    all_gather x1, blocking collectives, local(): halves = lax.all_gather(own, 'src', axis=0, axis_index_groups=far_pairs)  6.79 us
    all_gather x1, blocking collectives, local(): halves = lax.all_gather(halves, 'src', axis=0, axis_index_groups=pairs)  5.74 us
    all_gather x1, blocking collectives, local(): both = lax.all_gather(sums, 'src', axis=0, axis_index_groups=pairs)  5.2 us
    all_gather x1, blocking collectives, local(): both = lax.all_gather(averages, 'src', axis=0, axis_index_groups=pairs)  1.78 us
  transfers between devices with their start and end apart: 2, of which 1 were waited for; matrix products, arithmetic and copies ran while one was open for 0% of the time, Pallas kernels for 1%

profile of v9, /device:TPU:1, one launch (start us, length us, event | category | flops | bytes accessed | tf_op | source)
XLA Modules:
  0.0 67.6 jit_solution(14239051411706244355)
XLA Ops:
  0.6 0.0 copy-start.2
  0.6 11.5 %collective-permute-start = (bf16[64,256]{1,0:T(8,128)(2,1)}, bf16[64,256]{1,0:T(8,128)(2,1)S(1)}, u32[]{:S(2)}, u32[]{:S(2)}) collective-permute-start(bf16[64,256]{1,0:T(8,128)(2,1)} %bitcast.30), channel_id=1, source_target_pairs={{0,8},{1,9},{2,10},{3,11},{4,12},{5,13},{6,14},{7,15},{8,0},{9,1},... | collective-permute-start | bytes 98312 | tf_op jit(solution)/shard_map/ppermute | solution.py:102
  12.1 0.0 copy-done.2
  12.1 0.0 copy-start.3
  12.1 10.2 %conditional.1 = (bf16[8,32,256]{2,1,0:T(8,128)(2,1)S(1)}) conditional(s32[]{:T(128)} %convert_element_type.3, bf16[32,256]{1,0:T(8,128)(2,1)S(1)} %bitcast.28, bf16[32,256]{1,0:T(8,128)(2,1)S(1)} %bitcast.29), branch_computations={%region_0.1_spmd, %region_1.2_spmd} | conditional | bytes 409608 | solution.py:104
  12.2 10.2 %all_to_all.14 = bf16[8,32,256]{2,1,0:T(8,128)(2,1)S(1)} all-to-all(bf16[8,32,256]{2,1,0:T(8,128)(2,1)S(1)} %broadcast_in_dim.8), channel_id=1, replica_groups={{0,32,64,96,128,160,192,224},{16,48,80,112,144,176,208,240},{256,288,32..., dimensions={0} | all-to-all | bytes 262144 | tf_op jit(solution)/shard_map/cond/branch_1_fun/all_to_all | solution.py:106
  22.3 0.0 collective-permute-done
  22.3 0.0 copy-done.3
  22.3 0.8 %broadcast_in_dim.12 = bf16[8,2,64,256]{3,2,1,0:T(8,128)(2,1)} broadcast(bf16[2,64,256]{2,1,0:T(8,128)(2,1)S(1)} %pad_maximum_fusion), dimensions={1,2,3} | broadcast | bytes 589824 | tf_op jit(solution)/shard_map/broadcast_in_dim | solution.py:18
  23.2 6.8 %all-to-all-start.1 = ((bf16[8,2,64,256]{3,2,1,0:T(8,128)(2,1)}), bf16[8,2,64,256]{3,2,1,0:T(8,128)(2,1)S(1)}, u32[]{:S(2)}, u32[]{:S(2)}) async-start(bf16[8,2,64,256]{3,2,1,0:T(8,128)(2,1)} %broadcast_in_dim.12), calls=%async_computation.1 | async-start | bytes 1048576 | tf_op jit(solution)/shard_map/all_to_all | solution.py:112
  30.0 0.1 pad_add_fusion.start_ref
  30.1 6.8 %all-gather.1 = bf16[16,32,256]{2,1,0:T(8,128)(2,1)S(1)} all-gather(bf16[8,32,256]{2,1,0:T(8,128)(2,1)S(1)} %get-tuple-element.32), channel_id=3, replica_groups={{0,256},{16,272},{32,288},{48,304},{64,320},{80,336},{96,352},{112,368}..., dimensions={0}, use_global_device_ids=true | all-gather | bytes 393216 | tf_op jit(solution)/shard_map/all_gather | solution.py:114
  36.9 0.0 copy-start
  36.9 0.0 copy-start.1
  36.9 5.7 %all-gather.2 = bf16[4,8,32,256]{3,2,1,0:T(8,128)(2,1)S(1)} all-gather(bf16[2,8,32,256]{3,2,1,0:T(8,128)(2,1)S(1)} %bitcast.26), channel_id=4, replica_groups={{0,16},{32,48},{64,80},{96,112},{128,144},{160,176},{192,208},{224,240}..., dimensions={0}, use_global_device_ids=true | all-gather | bytes 786432 | tf_op jit(solution)/shard_map/all_gather | solution.py:115
  42.6 0.0 copy-done
  42.6 0.0 copy-done.1
  42.6 0.8 %shard_map.67 = (bf16[1024,256]{1,0:T(8,128)(2,1)S(1)}, f32[1,256]{1,0:T(1,128)S(1)}, s32[256,128]{1,0:T(8,128)S(1)}) custom-call(s32[3]{0:T(128)S(1)} %pad_add_fusion.start_ref, bf16[2,2,8,32,256]{4,3,2,1,0:T(8,128)(2,1)S(1)} %bitcast.21, s32[16,256]{1,0:T(8,128)S(1)} %bitcast.23, s32[16,256]{1,0:T(8,128)S(1)} %bitcast.24), custom_call_target="tpu_custom_call" | custom-call | flops 1000000 | bytes 1048576 | tf_op jit(solution)/shard_map/pallas_call | solution.py:119
  43.4 1.3 %all-to-all-done.1 = bf16[8,2,64,256]{3,2,1,0:T(8,128)(2,1)S(1)} async-done(((bf16[8,2,64,256]{3,2,1,0:T(8,128)(2,1)}), bf16[8,2,64,256]{3,2,1,0:T(8,128)(2,1)S(1)}, u32[]{:S(2)}, u32[]{:S(2)}) %all-to-all-start.1) | async-done | bytes 524320 | tf_op jit(solution)/shard_map/all_to_all | solution.py:112
  44.7 1.0 %shard_map.68 = (f32[256,256]{1,0:T(8,128)S(1)}, f32[2,256]{1,0:T(2,128)S(1)}) custom-call(bf16[1024,256]{1,0:T(8,128)(2,1)S(1)} %bitcast.22, bf16[1024,256]{1,0:T(8,128)(2,1)S(1)} %get-tuple-element.22.t_ref, f32[1,256]{1,0:T(1,128)S(1)} %get-tuple-element.23.scale_ref, s32[256,128]{1,0:T(8,128)S(1)} %get-tuple-element.24.lanes_ref), custom_call_target="tpu_custom_call" | custom-call | flops 300000000 | bytes 2097152 | tf_op jit(solution)/shard_map/pallas_call | solution.py:131
  45.8 5.2 %all-gather.5 = f32[2,2,256]{2,1,0:T(2,128)S(1)} all-gather(f32[1,2,256]{2,1,0:T(2,128)S(1)} %bitcast.25), channel_id=5, replica_groups={{0,16},{32,48},{64,80},{96,112},{128,144},{160,176},{192,208},{224,240}..., dimensions={0}, use_global_device_ids=true | all-gather | bytes 6144 | tf_op jit(solution)/shard_map/all_gather | solution.py:144
  51.0 13.8 %all_to_all.15 = f32[16,2,256]{2,1,0:T(2,128)S(1)} all-to-all(f32[16,2,256]{2,1,0:T(2,128)S(1)} %broadcast_in_dim.14), channel_id=1, replica_groups={{16,17,18,19,20,21,22,23,24,25,26,27,28,29,30,31},{48,49,50,51,52,53,54..., dimensions={0} | all-to-all | bytes 65536 | tf_op jit(solution)/shard_map/all_to_all | solution.py:146
  64.9 1.8 %all-gather.6.both_ref = f32[2,2,256]{2,1,0:T(2,128)S(1)} all-gather(f32[1,2,256]{2,1,0:T(2,128)S(1)} %multiply_bitcast_fusion), channel_id=6, replica_groups={{0,16},{32,48},{64,80},{96,112},{128,144},{160,176},{192,208},{224,240}..., dimensions={0}, use_global_device_ids=true | all-gather | bytes 6144 | tf_op jit(solution)/shard_map/all_gather | solution.py:148
  66.7 0.9 %shard_map.69 = (bf16[256,256]{1,0:T(8,128)(2,1)}, f32[1,256]{1,0:T(1,128)}, f32[1,256]{1,0:T(1,128)}) custom-call(s32[1]{0:T(128)} %bitcast.1.core_ref, f32[2,2,256]{2,1,0:T(2,128)S(1)} %all-gather.6.both_ref, f32[256,256]{1,0:T(8,128)S(1)} %get-tuple-element.26.cos_ref), custom_call_target="tpu_custom_call" | custom-call | flops 200000 | bytes 524288 | tf_op jit(solution)/shard_map/pallas_call | solution.py:149
  (7 shorter events, 0.1 us)
Async XLA Ops:
  0.6 11.5 %copy-start.2 = (bf16[256,32]{0,1:T(8,128)(2,1)S(1)}, bf16[256,32]{0,1:T(8,128)(2,1)}, u32[]{:S(2)}) copy-start(bf16[256,32]{0,1:T(8,128)(2,1)} %param.7) | copy-start | bytes 49156
  0.6 21.7 %collective-permute-start = (bf16[64,256]{1,0:T(8,128)(2,1)}, bf16[64,256]{1,0:T(8,128)(2,1)S(1)}, u32[]{:S(2)}, u32[]{:S(2)}) collective-permute-start(bf16[64,256]{1,0:T(8,128)(2,1)} %bitcast.30), channel_id=1, source_target_pairs={{0,8},{1,9},{2,10},{3,11},{4,12},{5,13},{6,14},{7,15},{8,0},{9,1},... | collective-permute-start | bytes 98312 | tf_op jit(solution)/shard_map/ppermute | solution.py:102
  12.1 10.2 %copy-start.3 = (bf16[256,64]{0,1:T(8,128)(2,1)S(1)}, bf16[256,64]{0,1:T(8,128)(2,1)}, u32[]{:S(2)}) copy-start(bf16[256,64]{0,1:T(8,128)(2,1)} %param.6) | copy-start | bytes 98308
  23.2 21.5 %all-to-all-start.1 = ((bf16[8,2,64,256]{3,2,1,0:T(8,128)(2,1)}), bf16[8,2,64,256]{3,2,1,0:T(8,128)(2,1)S(1)}, u32[]{:S(2)}, u32[]{:S(2)}) async-start(bf16[8,2,64,256]{3,2,1,0:T(8,128)(2,1)} %broadcast_in_dim.12), calls=%async_computation.1 | async-start | bytes 1048576 | tf_op jit(solution)/shard_map/all_to_all | solution.py:112
  36.9 5.7 %copy-start = (s32[256,16]{0,1:T(8,128)S(1)}, s32[256,16]{0,1:T(8,128)}, u32[]{:S(2)}) copy-start(s32[256,16]{0,1:T(8,128)} %param.8) | copy-start | bytes 49156
  36.9 5.7 %copy-start.1 = (s32[256,16]{0,1:T(8,128)S(1)}, s32[256,16]{0,1:T(8,128)}, u32[]{:S(2)}) copy-start(s32[256,16]{0,1:T(8,128)} %param.9) | copy-start | bytes 49156

commit v10 on v9

--- a/solution.py
+++ b/solution.py
@@ -108,7 +108,7 @@
         tgt_embed.T,
     )
     own, mine, partner = lax.optimization_barrier((own, mine, partner))
-    operand = spread(jnp.stack([mine, partner]), line)
+    operand = jnp.stack([spread(mine, line), spread(partner, line)], axis=1)
     source = lax.all_to_all(operand, "tgt", 0, 0, axis_index_groups=lines_y)
     source = source.reshape(-1, src_count)
     halves = lax.all_gather(own, "src", axis=0, axis_index_groups=far_pairs)

time: 68 us -> 68.8 us (1.012)
  other arithmetic: 0.15 us -> 0.98 us
    broadcast_in_dim x3 -> x2, local copies, waits for them, and re-layouts: 0.87 us -> 0.02 us  [spread(): return jnp.broadcast_to(values[None], (count,) + values.shape)]
    another operation x1, other arithmetic: 0.01 us -> 0.84 us  [local(): operand = jnp.stack([spread(mine, line), spread(partner, line)], axis=1)]
    unnamed x8, local copies, waits for them, and re-layouts: 0.02 us -> 0.74 us
where the time goes in v10:
time: 68.8 us; the launch traced here: 68.3 us
  blocking collectives  43.5 us (63%)
  starting transfers between devices  18.3 us (27%)
  Pallas kernels  2.73 us (4%)
  waiting for transfers between devices  1.33 us (2%)
  other arithmetic  0.98 us (1%)
  local copies, waits for them, and re-layouts  0.8 us (1%)
  between operations  0.69 us (1%)
    all_to_all x1, blocking collectives, local(): lax.all_to_all(spread(sums, chips), ('src', 'tgt'), 0, 0, axis_index_grou...  13.8 us
    ppermute x1, starting transfers between devices, local(): partner = lax.ppermute(mine, 'tgt', partners)  11.5 us
    all_to_all x1, blocking collectives, local(): lax.all_to_all(spread(part, copies), 'src', 0, 0, axis_index_groups=blocks)  10.2 us
    all_to_all x1, starting transfers between devices, local(): source = lax.all_to_all(operand, 'tgt', 0, 0, axis_index_groups=lines_y)  6.82 us
    all_gather x1, blocking collectives, local(): halves = lax.all_gather(own, 'src', axis=0, axis_index_groups=far_pairs)  6.79 us
    all_gather x1, blocking collectives, local(): halves = lax.all_gather(halves, 'src', axis=0, axis_index_groups=pairs)  5.74 us
    all_gather x1, blocking collectives, local(): both = lax.all_gather(sums, 'src', axis=0, axis_index_groups=pairs)  5.2 us
    all_gather x1, blocking collectives, local(): both = lax.all_gather(averages, 'src', axis=0, axis_index_groups=pairs)  1.78 us
  transfers between devices with their start and end apart: 2, of which 1 were waited for; matrix products, arithmetic and copies ran while one was open for 0% of the time, Pallas kernels for 1%

profile of v10, /device:TPU:1, one launch (start us, length us, event | category | flops | bytes accessed | tf_op | source)
XLA Modules:
  0.0 68.3 jit_solution(15368966558000993164)
XLA Ops:
  0.6 0.0 copy-start.2
  0.6 11.5 %collective-permute-start = (bf16[64,256]{1,0:T(8,128)(2,1)}, bf16[64,256]{1,0:T(8,128)(2,1)S(1)}, u32[]{:S(2)}, u32[]{:S(2)}) collective-permute-start(bf16[64,256]{1,0:T(8,128)(2,1)} %bitcast.28), channel_id=1, source_target_pairs={{0,8},{1,9},{2,10},{3,11},{4,12},{5,13},{6,14},{7,15},{8,0},{9,1},... | collective-permute-start | bytes 98312 | tf_op jit(solution)/shard_map/ppermute | solution.py:102
  12.1 0.0 copy-done.2
  12.1 10.2 %conditional.1 = (bf16[8,32,256]{2,1,0:T(8,128)(2,1)S(1)}) conditional(s32[]{:T(128)} %convert_element_type.3, bf16[32,256]{1,0:T(8,128)(2,1)S(1)} %bitcast.26, bf16[32,256]{1,0:T(8,128)(2,1)S(1)} %bitcast.27), branch_computations={%region_0.1_spmd, %region_1.2_spmd} | conditional | bytes 409608 | solution.py:104
  12.2 10.2 %all_to_all.14 = bf16[8,32,256]{2,1,0:T(8,128)(2,1)S(1)} all-to-all(bf16[8,32,256]{2,1,0:T(8,128)(2,1)S(1)} %broadcast_in_dim.3), channel_id=1, replica_groups={{0,32,64,96,128,160,192,224},{16,48,80,112,144,176,208,240},{256,288,32..., dimensions={0} | all-to-all | bytes 262144 | tf_op jit(solution)/shard_map/cond/branch_1_fun/all_to_all | solution.py:106
  22.3 0.0 copy-start.3
  22.3 0.0 collective-permute-done
  22.3 0.7 %copy-done.3 = bf16[256,64]{0,1:T(8,128)(2,1)S(1)} copy-done((bf16[256,64]{0,1:T(8,128)(2,1)S(1)}, bf16[256,64]{0,1:T(8,128)(2,1)}, u32[]{:S(2)}) %copy-start.3) | copy-done | bytes 32792
  23.1 0.8 %pad_maximum_fusion = bf16[8,2,64,256]{3,2,1,0:T(8,128)(2,1)} fusion(bf16[8,1,64,256]{3,2,1,0:T(8,128)(2,1)S(1)} %stack_broadcast_in_dim.5, bf16[8,1,64,256]{3,2,1,0:T(8,128)(2,1)S(1)} %stack_broadcast_in_dim.4), kind=kLoop, calls=%fused_computation | loop fusion | flops 262144 | bytes 1048576 | tf_op jit(solution)/shard_map/stack | solution.py:111
  23.9 6.8 %all-to-all-start.1 = ((bf16[8,2,64,256]{3,2,1,0:T(8,128)(2,1)}), bf16[8,2,64,256]{3,2,1,0:T(8,128)(2,1)S(1)}, u32[]{:S(2)}, u32[]{:S(2)}) async-start(bf16[8,2,64,256]{3,2,1,0:T(8,128)(2,1)} %pad_maximum_fusion), calls=%async_computation.1 | async-start | bytes 1048576 | tf_op jit(solution)/shard_map/all_to_all | solution.py:112
  30.8 0.1 pad_add_fusion.start_ref
  30.8 6.8 %all-gather.1 = bf16[16,32,256]{2,1,0:T(8,128)(2,1)S(1)} all-gather(bf16[8,32,256]{2,1,0:T(8,128)(2,1)S(1)} %get-tuple-element.32), channel_id=3, replica_groups={{0,256},{16,272},{32,288},{48,304},{64,320},{80,336},{96,352},{112,368}..., dimensions={0}, use_global_device_ids=true | all-gather | bytes 393216 | tf_op jit(solution)/shard_map/all_gather | solution.py:114
  37.6 0.0 copy-start
  37.6 0.0 copy-start.1
  37.6 5.7 %all-gather.2 = bf16[4,8,32,256]{3,2,1,0:T(8,128)(2,1)S(1)} all-gather(bf16[2,8,32,256]{3,2,1,0:T(8,128)(2,1)S(1)} %bitcast.24), channel_id=4, replica_groups={{0,16},{32,48},{64,80},{96,112},{128,144},{160,176},{192,208},{224,240}..., dimensions={0}, use_global_device_ids=true | all-gather | bytes 786432 | tf_op jit(solution)/shard_map/all_gather | solution.py:115
  43.4 0.0 copy-done
  43.4 0.0 copy-done.1
  43.4 0.8 %shard_map.67 = (bf16[1024,256]{1,0:T(8,128)(2,1)S(1)}, f32[1,256]{1,0:T(1,128)S(1)}, s32[256,128]{1,0:T(8,128)S(1)}) custom-call(s32[3]{0:T(128)S(1)} %pad_add_fusion.start_ref, bf16[2,2,8,32,256]{4,3,2,1,0:T(8,128)(2,1)S(1)} %bitcast.19, s32[16,256]{1,0:T(8,128)S(1)} %bitcast.21, s32[16,256]{1,0:T(8,128)S(1)} %bitcast.22), custom_call_target="tpu_custom_call" | custom-call | flops 1000000 | bytes 1048576 | tf_op jit(solution)/shard_map/pallas_call | solution.py:119
  44.2 1.3 %all-to-all-done.1 = bf16[8,2,64,256]{3,2,1,0:T(8,128)(2,1)S(1)} async-done(((bf16[8,2,64,256]{3,2,1,0:T(8,128)(2,1)}), bf16[8,2,64,256]{3,2,1,0:T(8,128)(2,1)S(1)}, u32[]{:S(2)}, u32[]{:S(2)}) %all-to-all-start.1) | async-done | bytes 524320 | tf_op jit(solution)/shard_map/all_to_all | solution.py:112
  45.5 1.0 %shard_map.68 = (f32[256,256]{1,0:T(8,128)S(1)}, f32[2,256]{1,0:T(2,128)S(1)}) custom-call(bf16[1024,256]{1,0:T(8,128)(2,1)S(1)} %bitcast.20, bf16[1024,256]{1,0:T(8,128)(2,1)S(1)} %get-tuple-element.22.t_ref, f32[1,256]{1,0:T(1,128)S(1)} %get-tuple-element.23.scale_ref, s32[256,128]{1,0:T(8,128)S(1)} %get-tuple-element.24.lanes_ref), custom_call_target="tpu_custom_call" | custom-call | flops 300000000 | bytes 2097152 | tf_op jit(solution)/shard_map/pallas_call | solution.py:131
  46.5 5.2 %all-gather.5 = f32[2,2,256]{2,1,0:T(2,128)S(1)} all-gather(f32[1,2,256]{2,1,0:T(2,128)S(1)} %bitcast.23), channel_id=5, replica_groups={{0,16},{32,48},{64,80},{96,112},{128,144},{160,176},{192,208},{224,240}..., dimensions={0}, use_global_device_ids=true | all-gather | bytes 6144 | tf_op jit(solution)/shard_map/all_gather | solution.py:144
  51.8 13.8 %all_to_all.15 = f32[16,2,256]{2,1,0:T(2,128)S(1)} all-to-all(f32[16,2,256]{2,1,0:T(2,128)S(1)} %broadcast_in_dim.11), channel_id=1, replica_groups={{16,17,18,19,20,21,22,23,24,25,26,27,28,29,30,31},{48,49,50,51,52,53,54..., dimensions={0} | all-to-all | bytes 65536 | tf_op jit(solution)/shard_map/all_to_all | solution.py:146
  65.6 1.8 %all-gather.6.both_ref = f32[2,2,256]{2,1,0:T(2,128)S(1)} all-gather(f32[1,2,256]{2,1,0:T(2,128)S(1)} %multiply_bitcast_fusion), channel_id=6, replica_groups={{0,16},{32,48},{64,80},{96,112},{128,144},{160,176},{192,208},{224,240}..., dimensions={0}, use_global_device_ids=true | all-gather | bytes 6144 | tf_op jit(solution)/shard_map/all_gather | solution.py:148
  67.4 0.9 %shard_map.69 = (bf16[256,256]{1,0:T(8,128)(2,1)}, f32[1,256]{1,0:T(1,128)}, f32[1,256]{1,0:T(1,128)}) custom-call(s32[1]{0:T(128)} %bitcast.1.core_ref, f32[2,2,256]{2,1,0:T(2,128)S(1)} %all-gather.6.both_ref, f32[256,256]{1,0:T(8,128)S(1)} %get-tuple-element.26.cos_ref), custom_call_target="tpu_custom_call" | custom-call | flops 200000 | bytes 524288 | tf_op jit(solution)/shard_map/pallas_call | solution.py:149
  (8 shorter events, 0.1 us)
Async XLA Ops:
  0.6 11.5 %copy-start.2 = (bf16[256,32]{0,1:T(8,128)(2,1)S(1)}, bf16[256,32]{0,1:T(8,128)(2,1)}, u32[]{:S(2)}) copy-start(bf16[256,32]{0,1:T(8,128)(2,1)} %param.7) | copy-start | bytes 49156
  0.6 21.7 %collective-permute-start = (bf16[64,256]{1,0:T(8,128)(2,1)}, bf16[64,256]{1,0:T(8,128)(2,1)S(1)}, u32[]{:S(2)}, u32[]{:S(2)}) collective-permute-start(bf16[64,256]{1,0:T(8,128)(2,1)} %bitcast.28), channel_id=1, source_target_pairs={{0,8},{1,9},{2,10},{3,11},{4,12},{5,13},{6,14},{7,15},{8,0},{9,1},... | collective-permute-start | bytes 98312 | tf_op jit(solution)/shard_map/ppermute | solution.py:102
  22.3 0.8 %copy-start.3 = (bf16[256,64]{0,1:T(8,128)(2,1)S(1)}, bf16[256,64]{0,1:T(8,128)(2,1)}, u32[]{:S(2)}) copy-start(bf16[256,64]{0,1:T(8,128)(2,1)} %param.6) | copy-start | bytes 98308
  23.9 21.5 %all-to-all-start.1 = ((bf16[8,2,64,256]{3,2,1,0:T(8,128)(2,1)}), bf16[8,2,64,256]{3,2,1,0:T(8,128)(2,1)S(1)}, u32[]{:S(2)}, u32[]{:S(2)}) async-start(bf16[8,2,64,256]{3,2,1,0:T(8,128)(2,1)} %pad_maximum_fusion), calls=%async_computation.1 | async-start | bytes 1048576 | tf_op jit(solution)/shard_map/all_to_all | solution.py:112
  37.6 5.7 %copy-start = (s32[256,16]{0,1:T(8,128)S(1)}, s32[256,16]{0,1:T(8,128)}, u32[]{:S(2)}) copy-start(s32[256,16]{0,1:T(8,128)} %param.8) | copy-start | bytes 49156
  37.6 5.7 %copy-start.1 = (s32[256,16]{0,1:T(8,128)S(1)}, s32[256,16]{0,1:T(8,128)}, u32[]{:S(2)}) copy-start(s32[256,16]{0,1:T(8,128)} %param.9) | copy-start | bytes 49156
